TPU v7x, 32 devices: a whole 2x2x4 slice. The times are simulated.
32 devices in a mesh: dp: 4 (over y, core), expert: 8 (over z, x).
Axes of the slice: x: 2, y: 2, z: 4, core: 2. Of those that a mesh axis runs over, the one named last changes fastest.
Arguments:
- tokens: bfloat16 [4096, 1024], P(('dp', 'expert')), may hold values from -6 to 6
- cotangent: bfloat16 [4096, 1024], P(('dp', 'expert')), may hold values from -6 to 6
- picks: int32 [32, 16], P(('dp', 'expert')), may hold values from 0 to 127
- gates: float32 [32, 16], P(('dp', 'expert')), may hold values from 0.1 to 1
- w_gate: bfloat16 [16, 2816, 1024], P('expert', 'dp'), may hold values from -0.1875 to 0.1875
- w_up: bfloat16 [16, 2816, 1024], P('expert', 'dp'), may hold values from -0.1875 to 0.1875
- w_down: bfloat16 [16, 2816, 1024], P('expert', 'dp'), may hold values from -0.109375 to 0.109375
Outputs:
- grad_tokens: bfloat16 [4096, 1024], P(('dp', 'expert'))
- grad_gate: bfloat16 [16, 2816, 1024], P('expert', 'dp')
- grad_up: bfloat16 [16, 2816, 1024], P('expert', 'dp')
- grad_down: bfloat16 [16, 2816, 1024], P('expert', 'dp')
Inputs may be any that keep to these rules, and one draw needn't show every extreme that they name: picks[s, e] is the row, among the 128 tokens of device s, that expert e takes from device s.
All inputs are finite; a program needn't handle non-finite values.
Results may differ from a plain program's by a relative error of at most 0.02.
Values may be sent and summed in bfloat16 or wider, within the bound.
A program may use at most 64 MiB of HBM per device.

v0:
```python
import jax
import jax.numpy as jnp
from jax import lax
from jax.sharding import PartitionSpec as P


def shards(tokens, cotangent, picks, gates, w_gate, w_up, w_down):
    expert_count = lax.axis_size("expert")
    token_rows, width = tokens.shape
    local_experts = w_gate.shape[0]
    chosen_row = picks[0]
    selector = (chosen_row[:, None] == jnp.arange(token_rows, dtype=jnp.int32)[None, :]).astype(
        jnp.bfloat16
    )
    chosen = jnp.dot(selector, tokens, preferred_element_type=jnp.float32).astype(jnp.bfloat16)
    picked_grad = jnp.dot(selector, cotangent, preferred_element_type=jnp.float32)
    scaled = (picked_grad * gates[0][:, None]).astype(jnp.bfloat16)
    layout = (expert_count, local_experts, width)
    got_x, got_dy = (
        lax.all_to_all(chosen.reshape(layout), "expert", split_axis=0, concat_axis=0, tiled=True),
        lax.all_to_all(scaled.reshape(layout), "expert", split_axis=0, concat_axis=0, tiled=True),
    )
    all_x, all_dy = (
        lax.all_gather(got_x, "dp", axis=0, tiled=True),
        lax.all_gather(got_dy, "dp", axis=0, tiled=True),
    )
    pre_gate = jnp.einsum("sed,efd->esf", all_x, w_gate, preferred_element_type=jnp.float32)
    pre_up = jnp.einsum("sed,efd->esf", all_x, w_up, preferred_element_type=jnp.float32)
    sigmoid_g = jax.nn.sigmoid(pre_gate)
    active = pre_gate * sigmoid_g
    hidden = (active * pre_up).astype(jnp.bfloat16)
    grad_hidden = jnp.einsum("sed,efd->esf", all_dy, w_down, preferred_element_type=jnp.float32)
    grad_down = jnp.einsum(
        "esf,sed->efd", hidden, all_dy, preferred_element_type=jnp.float32
    ).astype(jnp.bfloat16)
    d_up = (grad_hidden * active).astype(jnp.bfloat16)
    d_gate = (grad_hidden * pre_up * sigmoid_g * (1.0 + pre_gate * (1.0 - sigmoid_g))).astype(
        jnp.bfloat16
    )
    grad_gate = jnp.einsum(
        "esf,sed->efd", d_gate, all_x, preferred_element_type=jnp.float32
    ).astype(jnp.bfloat16)
    grad_up = jnp.einsum("esf,sed->efd", d_up, all_x, preferred_element_type=jnp.float32).astype(
        jnp.bfloat16
    )
    first = jnp.einsum("esf,efd->sed", d_gate, w_gate, preferred_element_type=jnp.float32)
    second = jnp.einsum("esf,efd->sed", d_up, w_up, preferred_element_type=jnp.float32)
    summed = lax.psum_scatter(
        (first + second).astype(jnp.bfloat16), "dp", scatter_dimension=0, tiled=True
    ).astype(jnp.float32)
    returned = lax.all_to_all(
        summed.astype(jnp.bfloat16), "expert", split_axis=0, concat_axis=0, tiled=True
    ).astype(summed.dtype)
    back_rows = returned.reshape(expert_count * local_experts, width)
    grad_tokens = jax.ops.segment_sum(back_rows, chosen_row, num_segments=token_rows).astype(
        jnp.bfloat16
    )
    return (grad_tokens, grad_gate, grad_up, grad_down)


def solution(mesh):
    return jax.shard_map(
        shards,
        mesh=mesh,
        in_specs=(
            P(("dp", "expert"), None),
            P(("dp", "expert"), None),
            P(("dp", "expert"), None),
            P(("dp", "expert"), None),
            P("expert", "dp", None),
            P("expert", "dp", None),
            P("expert", "dp", None),
        ),
        out_specs=(
            P(("dp", "expert"), None),
            P("expert", "dp", None),
            P("expert", "dp", None),
            P("expert", "dp", None),
        ),
        check_vma=False,
    )
```

profile of v0, /device:TPU:0, one launch (start us, length us, event | category | flops | bytes accessed | tf_op | source)
XLA Modules:
  0.0 88.1 jit_solution(107352284536867397)
XLA Ops:
  7.2 0.0 copy-start
  7.2 1.3 %convolution_convert_fusion.3 = bf16[16,1024]{1,0:T(8,128)(2,1)S(1)} fusion(bf16[128,1024]{1,0:T(8,128)(2,1)} %param.7, s32[16]{0:T(128)} %bitcast.27), kind=kOutput, calls=%fused_computation.9 | convolution fusion | flops 4212736 | bytes 294976 | tf_op jit(solution)/shard_map/dot_general | solution.py:15
  8.5 0.6 reshape.23
  9.1 7.3 %all-to-all-start.1 = ((bf16[8,2,1024]{2,1,0:T(2,128)(2,1)}), bf16[8,2,1024]{2,1,0:T(2,128)(2,1)S(1)}, u32[]{:S(2)}, u32[]{:S(2)}) async-start(bf16[8,2,1024]{2,1,0:T(2,128)(2,1)} %reshape.23), calls=%async_computation.1 | async-start | bytes 65536 | tf_op jit(solution)/shard_map/all_to_all | solution.py:20
  16.4 1.1 %fusion.2 = bf16[16,1024]{1,0:T(8,128)(2,1)S(1)} fusion(bf16[128,1024]{1,0:T(8,128)(2,1)} %param.8, f32[16]{0:T(128)} %bitcast.30, s32[16]{0:T(128)} %bitcast.28), kind=kOutput, calls=%fused_computation.8 | convolution fusion | flops 4229120 | bytes 295040 | tf_op jit(solution)/shard_map/dot_general | solution.py:16
  17.5 0.6 reshape.22
  18.2 4.9 %all-to-all-done.1 = bf16[8,2,1024]{2,1,0:T(2,128)(2,1)S(1)} async-done(((bf16[8,2,1024]{2,1,0:T(2,128)(2,1)}), bf16[8,2,1024]{2,1,0:T(2,128)(2,1)S(1)}, u32[]{:S(2)}, u32[]{:S(2)}) %all-to-all-start.1) | async-done | bytes 32800 | tf_op jit(solution)/shard_map/all_to_all | solution.py:20
  23.1 3.3 %all-to-all-start = ((bf16[8,2,1024]{2,1,0:T(2,128)(2,1)}), bf16[8,2,1024]{2,1,0:T(2,128)(2,1)S(1)}, u32[]{:S(2)}, u32[]{:S(2)}) async-start(bf16[8,2,1024]{2,1,0:T(2,128)(2,1)} %reshape.22), calls=%async_computation | async-start | bytes 65536 | tf_op jit(solution)/shard_map/all_to_all | solution.py:21
  26.4 0.0 reduce-scatter.4.cloned.1.call-start
  26.5 5.4 %all_gather.7 = bf16[32,2,1024]{2,0,1:T(8,128)(2,1)S(1)} all-gather(bf16[8,2,1024]{2,0,1:T(8,128)(2,1)S(1)} %copy.17), channel_id=1, replica_groups=mesh['dp'=4,'expert'=8] {'dp'}, dimensions={0}, use_global_device_ids=true | all-gather | bytes 163840 | tf_op jit(solution)/shard_map/all_gather | solution.py:24
  31.9 1.1 %all-to-all-done = bf16[8,2,1024]{2,1,0:T(2,128)(2,1)S(1)} async-done(((bf16[8,2,1024]{2,1,0:T(2,128)(2,1)}), bf16[8,2,1024]{2,1,0:T(2,128)(2,1)S(1)}, u32[]{:S(2)}, u32[]{:S(2)}) %all-to-all-start) | async-done | bytes 32800 | tf_op jit(solution)/shard_map/all_to_all | solution.py:21
  33.0 0.0 copy-start.1
  33.1 5.6 %all_gather.6 = bf16[32,2,1024]{2,0,1:T(8,128)(2,1)S(1)} all-gather(bf16[8,2,1024]{2,0,1:T(8,128)(2,1)S(1)} %copy.16), channel_id=1, replica_groups=mesh['dp'=4,'expert'=8] {'dp'}, dimensions={0}, use_global_device_ids=true | all-gather | bytes 163840 | tf_op jit(solution)/shard_map/all_gather | solution.py:25
  38.6 0.0 copy-done
  38.6 0.9 %fusion.11 = f32[2,32,704]{2,1,0:T(8,128)S(1)} fusion(bf16[32,2,1024]{2,0,1:T(8,128)(2,1)S(1)} %all_gather.7, bf16[2,704,1024]{2,1,0:T(8,128)(2,1)S(1)} %copy-done), kind=kOutput, calls=%fused_computation.22 | convolution fusion | flops 92274688 | bytes 3194880 | tf_op jit(solution)/shard_map/sed,efd->esf/dot_general | solution.py:27
  39.5 0.0 copy-done.1
  39.6 0.0 copy-start.2
  39.6 0.9 %fusion.10 = f32[2,32,704]{2,1,0:T(8,128)S(1)} fusion(bf16[32,2,1024]{2,0,1:T(8,128)(2,1)S(1)} %all_gather.7, bf16[2,704,1024]{2,1,0:T(8,128)(2,1)S(1)} %copy-done.1), kind=kOutput, calls=%fused_computation.21 | convolution fusion | flops 92274688 | bytes 3194880 | tf_op jit(solution)/shard_map/sed,efd->esf/dot_general | solution.py:28
  40.5 2.6 %convolution_convert_fusion = bf16[2,704,1024]{2,1,0:T(8,128)(2,1)} fusion(bf16[32,2,1024]{2,0,1:T(8,128)(2,1)S(1)} %all_gather.6, f32[2,32,704]{2,1,0:T(8,128)S(1)} %fusion.10, f32[2,32,704]{2,1,0:T(8,128)S(1)} %fusion.11), kind=kOutput, calls=%fused_computation.1 | convolution fusion | flops 93986816 | bytes 3375104 | tf_op jit(solution)/shard_map/esf,sed->efd/dot_general | solution.py:33
  43.0 0.0 copy-done.2
  43.0 0.9 %multiply_convert_fusion.1 = (bf16[2,32,704]{2,1,0:T(8,128)(2,1)S(1)}, bf16[2,32,704]{2,1,0:T(8,128)(2,1)S(1)}) fusion(f32[2,32,704]{2,1,0:T(8,128)S(1)} %fusion.11, f32[2,32,704]{2,1,0:T(8,128)S(1)} %fusion.10, bf16[32,2,1024]{2,0,1:T(8,128)(2,1)S(1)} %all_gather.6, bf16[2,704,1024]{2,1,0:T(8,128)(2,1)S(1)} %copy-done.2), kind=kOutput, calls=%fused_computation.13 | convolution fusion | flops 92860416 | bytes 3555328 | tf_op jit(solution)/shard_map/sed,efd->esf/dot_general | solution.py:32
  44.0 0.6 fusion.12
  44.6 0.6 fusion.1
  45.2 0.7 copy.21
  45.9 0.0 reduce-scatter.4.cloned.1.call-update
  45.9 2.5 %convolution_convert_fusion.1 = bf16[2,704,1024]{2,1,0:T(8,128)(2,1)} fusion(bf16[2,32,704]{2,1,0:T(8,128)(2,1)S(1)} %get-tuple-element.4, bf16[32,2,1024]{2,0,1:T(8,128)(2,1)S(1)} %all_gather.7), kind=kOutput, calls=%fused_computation.2 | convolution fusion | flops 93716480 | bytes 3104768 | tf_op jit(solution)/shard_map/esf,sed->efd/dot_general | solution.py:43
  48.5 17.4 %reduce-scatter.4.cloned.1.call-done = bf16[8,2048]{1,0:T(8,128)(2,1)} async-done(((bf16[32,2048]{1,0:T(8,128)(2,1)}), bf16[8,2048]{1,0:T(8,128)(2,1)}) %reduce-scatter.4.cloned.1.call-update) | async-done | bytes 32784
  65.9 1.4 %copy.18 = bf16[8,2,1024]{2,1,0:T(2,128)(2,1)} copy(bf16[8,2,1024]{2,0,1:T(8,128)(2,1)} %bitcast.26) | data formatting | bytes 65536 | tf_op jit(solution)/shard_map/reduce_scatter | solution.py:48
  67.3 5.5 %all-to-all-start.2 = ((bf16[8,2,1024]{2,1,0:T(2,128)(2,1)}), bf16[8,2,1024]{2,1,0:T(2,128)(2,1)S(1)}, u32[]{:S(2)}, u32[]{:S(2)}) async-start(bf16[8,2,1024]{2,1,0:T(2,128)(2,1)} %copy.18), calls=%async_computation.2 | async-start | bytes 65536 | tf_op jit(solution)/shard_map/all_to_all | solution.py:51
  72.8 2.5 %convolution_convert_fusion.2 = bf16[2,704,1024]{2,1,0:T(8,128)(2,1)} fusion(bf16[2,32,704]{2,1,0:T(8,128)(2,1)S(1)} %get-tuple-element.5, bf16[32,2,1024]{2,0,1:T(8,128)(2,1)S(1)} %all_gather.7), kind=kOutput, calls=%fused_computation.3 | convolution fusion | flops 93716480 | bytes 3104768 | tf_op jit(solution)/shard_map/esf,sed->efd/dot_general | solution.py:40
  75.3 4.2 %all-to-all-done.2 = bf16[8,2,1024]{2,1,0:T(2,128)(2,1)S(1)} async-done(((bf16[8,2,1024]{2,1,0:T(2,128)(2,1)}), bf16[8,2,1024]{2,1,0:T(2,128)(2,1)S(1)}, u32[]{:S(2)}, u32[]{:S(2)}) %all-to-all-start.2) | async-done | bytes 32800 | tf_op jit(solution)/shard_map/all_to_all | solution.py:51
  79.5 1.0 %scatter_custom_fusion = f32[128,1024]{1,0:T(8,128)S(1)} fusion(s32[16]{0:T(128)} %bitcast.29, f32[16,1024]{1,0:T(8,128)S(1)} %reshape.32, f32[]{:T(128)} %constant.0.clone.1), kind=kCustom, calls=%fused_computation.10 | custom fusion | flops 16384 | bytes 524800 | tf_op jit(solution)/shard_map/scatter-add | solution.py:55
  80.5 0.7 convert_element_type.43
  (3 shorter events, 0.0 us)
Async XLA Ops:
  7.2 31.5 %copy-start = (bf16[2,704,1024]{2,1,0:T(8,128)(2,1)S(1)}, bf16[2,704,1024]{2,1,0:T(8,128)(2,1)}, u32[]{:S(2)}) copy-start(bf16[2,704,1024]{2,1,0:T(8,128)(2,1)} %param.11) | copy-start | bytes 8650756
  9.1 13.9 %all-to-all-start.1 = ((bf16[8,2,1024]{2,1,0:T(2,128)(2,1)}), bf16[8,2,1024]{2,1,0:T(2,128)(2,1)S(1)}, u32[]{:S(2)}, u32[]{:S(2)}) async-start(bf16[8,2,1024]{2,1,0:T(2,128)(2,1)} %reshape.23), calls=%async_computation.1 | async-start | bytes 65536 | tf_op jit(solution)/shard_map/all_to_all | solution.py:20
  23.1 10.0 %all-to-all-start = ((bf16[8,2,1024]{2,1,0:T(2,128)(2,1)}), bf16[8,2,1024]{2,1,0:T(2,128)(2,1)S(1)}, u32[]{:S(2)}, u32[]{:S(2)}) async-start(bf16[8,2,1024]{2,1,0:T(2,128)(2,1)} %reshape.22), calls=%async_computation | async-start | bytes 65536 | tf_op jit(solution)/shard_map/all_to_all | solution.py:21
  26.4 39.5 %reduce-scatter.4.cloned.1.call-start = ((), (), s32[]{:S(2)}) async-start(), calls=%async_computation.4 | async-start | bytes 163840
  33.0 6.5 %copy-start.1 = (bf16[2,704,1024]{2,1,0:T(8,128)(2,1)S(1)}, bf16[2,704,1024]{2,1,0:T(8,128)(2,1)}, u32[]{:S(2)}) copy-start(bf16[2,704,1024]{2,1,0:T(8,128)(2,1)} %param.12) | copy-start | bytes 8650756
  39.6 3.5 %copy-start.2 = (bf16[2,704,1024]{2,1,0:T(8,128)(2,1)S(1)}, bf16[2,704,1024]{2,1,0:T(8,128)(2,1)}, u32[]{:S(2)}) copy-start(bf16[2,704,1024]{2,1,0:T(8,128)(2,1)} %param.13) | copy-start | bytes 8650756
  67.3 12.2 %all-to-all-start.2 = ((bf16[8,2,1024]{2,1,0:T(2,128)(2,1)}), bf16[8,2,1024]{2,1,0:T(2,128)(2,1)S(1)}, u32[]{:S(2)}, u32[]{:S(2)}) async-start(bf16[8,2,1024]{2,1,0:T(2,128)(2,1)} %copy.18), calls=%async_computation.2 | async-start | bytes 65536 | tf_op jit(solution)/shard_map/all_to_all | solution.py:51
Sparse Core Ops, SparseCore 0:
  46.0 19.8 reduce-scatter.3
where the time goes:
time: 88.5 us; the launch traced here: 88.1 us
  waiting for transfers between devices  27.6 us (31%)
  starting transfers between devices  16.2 us (18%)
  matrix products  14.1 us (16%)
  between operations  14.1 us (16%)
  blocking collectives  11 us (12%)
  local copies, waits for them, and re-layouts  3.42 us (4%)
  other arithmetic  1.71 us (2%)
    unnamed x2, waiting for transfers between devices  17.4 us
    all_to_all x1, starting transfers between devices, shards(): lax.all_to_all(chosen.reshape(layout), 'expert', split_axis=0, concat_axi...  7.25 us
    all_gather x1, blocking collectives, shards(): lax.all_gather(got_dy, 'dp', axis=0, tiled=True)  5.56 us
    all_to_all x1, starting transfers between devices, shards(): lax.all_to_all(summed.astype(jnp.bfloat16), 'expert', split_axis=0, conca...  5.52 us
    all_gather x1, blocking collectives, shards(): lax.all_gather(got_x, 'dp', axis=0, tiled=True)  5.43 us
    all_to_all x1, waiting for transfers between devices, shards(): lax.all_to_all(chosen.reshape(layout), 'expert', split_axis=0, concat_axi...  4.89 us
    all_to_all x1, waiting for transfers between devices, shards(): lax.all_to_all(summed.astype(jnp.bfloat16), 'expert', split_axis=0, conca...  4.15 us
    all_to_all x1, starting transfers between devices, shards(): lax.all_to_all(scaled.reshape(layout), 'expert', split_axis=0, concat_axi...  3.34 us
  transfers between devices with their start and end apart: 4, of which 4 were waited for; matrix products, arithmetic and copies ran while one was open for 8% of the time, Pallas kernels for 0%

commit v1 on v0

v1 whole, which is shorter than its diff:
```python
import functools

import jax
import jax.numpy as jnp
from jax import lax
from jax.experimental import pallas as pl
from jax.experimental.pallas import tpu as pltpu
from jax.sharding import PartitionSpec as P

LANES = 128
BF16 = jnp.bfloat16
F32 = jnp.float32
NT = (((1,), (1,)), ((), ()))


def bulk_wait(ref, count, sem):
    part = ref.at[pl.ds(0, count)]
    pltpu.make_async_copy(part, part, sem).wait()


def exchange_kernel(
    n_dp,
    n_ex,
    picks_ref,
    gates_ref,
    tokens_hbm,
    cot_hbm,
    wg_hbm,
    wu_hbm,
    wd_hbm,
    x_out,
    dy_out,
    dt_out,
    back_out,
    tok,
    cot,
    wg,
    wu,
    wd,
    wide,
    xmsg,
    dymsg,
    xbuf,
    dybuf,
    partmsg,
    backbuf,
    load_sem,
    send_sem,
    recv_sem,
):
    n = n_dp * n_ex
    experts, _, width = wg.shape
    chunks = width // LANES
    picked = picks_ref.shape[1]
    token_rows = tok.shape[0]
    rows = n * experts
    my_dp, my_ex = lax.axis_index("dp"), lax.axis_index("expert")
    me = my_dp * n_ex + my_ex

    loads = [
        pltpu.make_async_copy(src, dst, load_sem.at[i])
        for i, (src, dst) in enumerate(
            ((tokens_hbm, tok), (cot_hbm, cot), (wg_hbm, wg), (wu_hbm, wu), (wd_hbm, wd))
        )
    ]
    for load in loads:
        load.start()

    def peer(step):
        other = lax.rem(me + step, n)
        return other, (other // n_ex, lax.rem(other, n_ex))

    barrier = pltpu.get_barrier_semaphore()

    def greet(step, carry):
        _, where = peer(step)
        pl.semaphore_signal(
            barrier, inc=1, device_id=where, device_id_type=pl.DeviceIdType.MESH
        )
        return carry

    lax.fori_loop(1, n, greet, 0)

    eye = lax.broadcasted_iota(jnp.int32, (picked, picked), 0) == lax.broadcasted_iota(
        jnp.int32, (picked, picked), 1
    )
    pick_col = jnp.sum(
        jnp.where(eye, picks_ref[...].astype(F32), 0.0), axis=1, keepdims=True
    ).astype(jnp.int32)
    gate_col = jnp.sum(jnp.where(eye, gates_ref[...], 0.0), axis=1, keepdims=True)
    selector = jnp.where(
        lax.broadcasted_iota(jnp.int32, (picked, token_rows), 1) == pick_col, 1.0, 0.0
    ).astype(BF16)

    def pack(value, msg):
        count = value.shape[0]
        for k in range(chunks):
            wide[pl.ds(k, count, stride=chunks), :] = value[:, k * LANES : (k + 1) * LANES]
        msg[...] = wide[pl.ds(0, count * chunks), :].astype(BF16).reshape(msg.shape)

    def unpack(buf, out):
        wide[...] = buf[...].reshape(wide.shape).astype(F32)
        for k in range(chunks):
            out[:, k * LANES : (k + 1) * LANES] = wide[pl.ds(k, rows, stride=chunks), :].astype(
                BF16
            )

    def send_all(msg, buf, slot, by_expert):
        def one(step, carry):
            other, where = peer(step)
            pltpu.make_async_remote_copy(
                src_ref=msg.at[where[1] if by_expert else other],
                dst_ref=buf.at[me],
                send_sem=send_sem.at[slot],
                recv_sem=recv_sem.at[slot],
                device_id=where,
                device_id_type=pl.DeviceIdType.MESH,
            ).start()
            return carry

        lax.fori_loop(1, n, one, 0)
        buf[me] = msg[my_ex if by_expert else me]

    loads[0].wait()
    pack(jnp.dot(selector, tok[...], preferred_element_type=F32), xmsg)
    pl.semaphore_wait(barrier, n - 1)
    send_all(xmsg, xbuf, 0, True)
    loads[1].wait()
    pack(jnp.dot(selector, cot[...], preferred_element_type=F32) * gate_col, dymsg)
    send_all(dymsg, dybuf, 1, True)

    expert_of = lax.rem(lax.broadcasted_iota(jnp.int32, (rows, 1), 0), experts)

    def forward(value, weights):
        total = lax.dot_general(value, weights[0], NT, preferred_element_type=F32)
        for e in range(1, experts):
            total = jnp.where(
                expert_of == e,
                lax.dot_general(value, weights[e], NT, preferred_element_type=F32),
                total,
            )
        return total

    bulk_wait(xbuf, n - 1, recv_sem.at[0])
    unpack(xbuf, x_out)
    x = x_out[...]
    loads[2].wait()
    pre_gate = forward(x, wg)
    loads[3].wait()
    pre_up = forward(x, wu)
    sigmoid_g = jax.nn.sigmoid(pre_gate)
    active = pre_gate * sigmoid_g
    hidden = active * pre_up
    slope = pre_up * sigmoid_g * (1.0 + pre_gate * (1.0 - sigmoid_g))
    loads[4].wait()
    bulk_wait(dybuf, n - 1, recv_sem.at[1])
    unpack(dybuf, dy_out)
    grad_hidden = forward(dy_out[...], wd)
    d_up = grad_hidden * active
    d_gate = grad_hidden * slope

    part = jnp.zeros((rows, width), F32)
    for e in range(experts):
        mine = expert_of == e
        part += jnp.dot(
            jnp.where(mine, d_gate, 0.0).astype(BF16), wg[e], preferred_element_type=F32
        )
        part += jnp.dot(
            jnp.where(mine, d_up, 0.0).astype(BF16), wu[e], preferred_element_type=F32
        )
    pack(part, partmsg)
    send_all(partmsg, backbuf, 2, False)
    dt_out[0] = d_gate.T.astype(BF16)
    dt_out[1] = d_up.T.astype(BF16)
    dt_out[2] = hidden.T.astype(BF16)
    bulk_wait(backbuf, n - 1, recv_sem.at[2])
    unpack(backbuf, back_out)
    bulk_wait(xbuf, n - 1, send_sem.at[0])
    bulk_wait(dybuf, n - 1, send_sem.at[1])
    bulk_wait(partmsg, n - 1, send_sem.at[2])


def grads_kernel(
    n_dp, experts, picks_ref, back_ref, x_ref, dy_ref, dt_ref, tokens_out, gate_out, up_out, down_out
):
    expert = pl.program_id(0)

    @pl.when((expert == 0) & (pl.program_id(1) == 0))
    def _():
        shape = (tokens_out.shape[0], picks_ref.shape[1])
        chosen = jnp.where(
            lax.broadcasted_iota(jnp.int32, shape, 0) == picks_ref[...], 1.0, 0.0
        )
        spread = jnp.concatenate([chosen] * n_dp, axis=1).astype(BF16)
        tokens_out[...] = jnp.dot(
            spread, back_ref[...], preferred_element_type=F32
        ).astype(BF16)

    rows = x_ref.shape[0]
    lane = lax.broadcasted_iota(jnp.int32, (1, rows), 1)
    mine = jnp.where(lax.rem(lane, experts) == expert, 1.0, 0.0).astype(BF16)
    for i, (out, other) in enumerate(((gate_out, x_ref), (up_out, x_ref), (down_out, dy_ref))):
        out[0] = jnp.dot(dt_ref[i] * mine, other[...], preferred_element_type=F32).astype(BF16)


def shards(n_dp, n_ex, tokens, cotangent, picks, gates, w_gate, w_up, w_down):
    token_rows, width = tokens.shape
    experts, hidden, _ = w_gate.shape
    n = n_dp * n_ex
    rows = n * experts
    message = (experts * width // LANES, LANES)
    weight = pltpu.VMEM((experts, hidden, width), BF16)
    vmem = pl.BlockSpec(memory_space=pltpu.VMEM)
    anywhere = pl.BlockSpec(memory_space=pl.ANY)
    x, dy, dt, back = pl.pallas_call(
        functools.partial(exchange_kernel, n_dp, n_ex),
        out_shape=(
            jax.ShapeDtypeStruct((rows, width), BF16),
            jax.ShapeDtypeStruct((rows, width), BF16),
            jax.ShapeDtypeStruct((3, hidden, rows), BF16),
            jax.ShapeDtypeStruct((rows, width), BF16),
        ),
        in_specs=[vmem] * 2 + [anywhere] * 5,
        out_specs=(vmem,) * 4,
        scratch_shapes=[
            pltpu.VMEM((token_rows, width), BF16),
            pltpu.VMEM((token_rows, width), BF16),
            weight,
            weight,
            weight,
            pltpu.VMEM((rows * width // LANES, LANES), F32),
            pltpu.VMEM((n_ex,) + message, BF16),
            pltpu.VMEM((n_ex,) + message, BF16),
            pltpu.VMEM((n,) + message, BF16),
            pltpu.VMEM((n,) + message, BF16),
            pltpu.VMEM((n,) + message, BF16),
            pltpu.VMEM((n,) + message, BF16),
            pltpu.SemaphoreType.DMA((5,)),
            pltpu.SemaphoreType.DMA((3,)),
            pltpu.SemaphoreType.DMA((3,)),
        ],
        compiler_params=pltpu.CompilerParams(
            collective_id=0, has_side_effects=True, vmem_limit_bytes=56 * 1024 * 1024
        ),
    )(picks, gates, tokens, cotangent, w_gate, w_up, w_down)

    step = max(d for d in range(16, 177, 16) if hidden % d == 0)
    whole = lambda *shape: pl.BlockSpec(shape, lambda e, f: (0,) * len(shape))
    tile = pl.BlockSpec((1, step, width), lambda e, f: (e, f, 0))
    grad = jax.ShapeDtypeStruct(w_gate.shape, BF16)
    return pl.pallas_call(
        functools.partial(grads_kernel, n_dp, experts),
        grid=(experts, hidden // step),
        out_shape=(jax.ShapeDtypeStruct(tokens.shape, BF16), grad, grad, grad),
        in_specs=[
            whole(*picks.shape),
            whole(rows, width),
            whole(rows, width),
            whole(rows, width),
            pl.BlockSpec((3, step, rows), lambda e, f: (0, f, 0)),
        ],
        out_specs=(whole(*tokens.shape), tile, tile, tile),
        compiler_params=pltpu.CompilerParams(vmem_limit_bytes=48 * 1024 * 1024),
    )(picks, back, x, dy, dt)


def solution(mesh):
    spread = P(("dp", "expert"), None)
    weight = P("expert", "dp", None)
    return jax.shard_map(
        functools.partial(shards, mesh.shape["dp"], mesh.shape["expert"]),
        mesh=mesh,
        in_specs=(spread,) * 4 + (weight,) * 3,
        out_specs=(spread,) + (weight,) * 3,
        check_vma=False,
    )
```

time: 88.5 us -> 35.2 us (0.40)
  Pallas kernels: 0 us -> 30.5 us
  waiting for transfers between devices: 27.6 us -> 0 us
  starting transfers between devices: 16.2 us -> 0 us
  matrix products: 14.1 us -> 0 us
  between operations: 14.1 us -> 0.67 us
  blocking collectives: 11 us -> 0 us
  other arithmetic: 1.71 us -> 0 us
    pallas_call x0 -> x2, Pallas kernels: none -> 30.5 us  [the longest x1 24.5 us: shards(): pl.pallas_call(functools.partial(exchange_kernel, n_dp, n_ex), out_shape=...]
    unnamed x2 -> x0, waiting for transfers between devices: 17.4 us -> none
    all_to_all x3 -> x0, starting transfers between devices: 16.1 us -> none  [the longest x1 7.25 us: shards(): lax.all_to_all(chosen.reshape(layout), 'expert', split_axis=0, concat_axi...]
    dot_general x10 -> x0, matrix products: 14.1 us -> none  [the longest x1 2.56 us: shards(): jnp.einsum('esf,sed->efd', hidden, all_dy, preferred_element_type=jnp.flo...]
    all_gather x2 -> x0, blocking collectives: 11 us -> none  [the longest x1 5.56 us: shards(): lax.all_gather(got_dy, 'dp', axis=0, tiled=True)]
    all_to_all x3 -> x0, waiting for transfers between devices: 10.2 us -> none  [the longest x1 4.89 us: shards(): lax.all_to_all(chosen.reshape(layout), 'expert', split_axis=0, concat_axi...]
    unnamed x7 -> x10, local copies, waits for them, and re-layouts: 0.7 us -> 3.76 us
    reduce_scatter x1 -> x0, local copies, waits for them, and re-layouts: 1.41 us -> none  [shards(): lax.psum_scatter((first + second).astype(jnp.bfloat16), 'dp', scatter_dim...]
  transfers between devices with their start and end apart: 4 -> 0, of which waited for: 4 -> 0; matrix products, arithmetic and copies ran while one was open for 8% -> 0% of each run, Pallas kernels for 0% -> 0%
where the time goes in v1:
time: 35.2 us; the launch traced here: 34.9 us
  Pallas kernels  30.5 us (87%)
  local copies, waits for them, and re-layouts  3.76 us (11%)
  between operations  0.67 us (2%)
    pallas_call x1, Pallas kernels, shards(): pl.pallas_call(functools.partial(exchange_kernel, n_dp, n_ex), out_shape=...  24.5 us
    pallas_call x1, Pallas kernels, shards(): pl.pallas_call(functools.partial(grads_kernel, n_dp, experts), grid=(expe...  6.03 us
    unnamed x10, local copies, waits for them, and re-layouts  3.76 us

profile of v1, /device:TPU:0, one launch (start us, length us, event | category | flops | bytes accessed | tf_op | source)
XLA Modules:
  0.0 34.9 jit_solution(17729086982888100809)
XLA Ops:
  0.6 0.0 copy-start.4
  0.6 24.5 %shard_map.102 = (bf16[64,1024]{1,0:T(8,128)(2,1)}, bf16[64,1024]{1,0:T(8,128)(2,1)}, bf16[3,704,64]{2,1,0:T(8,128)(2,1)}, bf16[64,1024]{1,0:T(8,128)(2,1)}) custom-call(s32[1,16]{1,0:T(1,128)} %picks_ref.3, f32[1,16]{1,0:T(1,128)} %gates_ref.1, bf16[128,1024]{1,0:T(8,128)(2,1)} %tokens_hbm.1, bf16[128,1024]{1,0:T(8,128)(2,1)} %cot_hbm.1, ...), custom_call_target="tpu_custom_call" | custom-call | tf_op jit(solution)/shard_map/pallas_call | solution.py:215
  25.1 0.0 copy-done.4
  25.2 0.0 copy-start
  25.2 1.0 %copy-done = bf16[3,704,64]{2,1,0:T(8,128)(2,1)S(1)} copy-done((bf16[3,704,64]{2,1,0:T(8,128)(2,1)S(1)}, bf16[3,704,64]{2,1,0:T(8,128)(2,1)}, u32[]{:S(2)}) %copy-start) | copy-done | bytes 270360
  26.2 0.0 copy-start.1
  26.2 0.9 %copy-done.1 = bf16[64,1024]{1,0:T(8,128)(2,1)S(1)} copy-done((bf16[64,1024]{1,0:T(8,128)(2,1)S(1)}, bf16[64,1024]{1,0:T(8,128)(2,1)}, u32[]{:S(2)}) %copy-start.1) | copy-done | bytes 131096
  27.1 0.0 copy-start.2
  27.1 0.9 %copy-done.2 = bf16[64,1024]{1,0:T(8,128)(2,1)S(1)} copy-done((bf16[64,1024]{1,0:T(8,128)(2,1)S(1)}, bf16[64,1024]{1,0:T(8,128)(2,1)}, u32[]{:S(2)}) %copy-start.2) | copy-done | bytes 131096
  28.0 0.0 copy-start.3
  28.0 0.9 %copy-done.3 = bf16[64,1024]{1,0:T(8,128)(2,1)S(1)} copy-done((bf16[64,1024]{1,0:T(8,128)(2,1)S(1)}, bf16[64,1024]{1,0:T(8,128)(2,1)}, u32[]{:S(2)}) %copy-start.3) | copy-done | bytes 131096
  28.9 6.0 %shard_map.103 = (bf16[128,1024]{1,0:T(8,128)(2,1)}, bf16[2,704,1024]{2,1,0:T(8,128)(2,1)}, bf16[2,704,1024]{2,1,0:T(8,128)(2,1)}, bf16[2,704,1024]{2,1,0:T(8,128)(2,1)}) custom-call(s32[1,16]{1,0:T(1,128)S(1)} %copy-done.4, bf16[64,1024]{1,0:T(8,128)(2,1)S(1)} %copy-done.3, bf16[64,1024]{1,0:T(8,128)(2,1)S(1)} %copy-done.1, bf16[64,1024]{1,0:T(8,128)(2,1)S(1)} %copy-done.2, ...), custom_call_target="tpu_custom_call" | custom-call | tf_op jit(solution)/shard_map/pallas_call | solution.py:251
Async XLA Ops:
  0.6 24.5 %copy-start.4 = (s32[1,16]{1,0:T(1,128)S(1)}, s32[1,16]{1,0:T(1,128)}, u32[]{:S(2)}) copy-start(s32[1,16]{1,0:T(1,128)} %picks_ref.3) | copy-start | bytes 196
  25.2 1.0 %copy-start = (bf16[3,704,64]{2,1,0:T(8,128)(2,1)S(1)}, bf16[3,704,64]{2,1,0:T(8,128)(2,1)}, u32[]{:S(2)}) copy-start(bf16[3,704,64]{2,1,0:T(8,128)(2,1)} %get-tuple-element.11.dt_ref) | copy-start | bytes 811012
  26.2 0.9 %copy-start.1 = (bf16[64,1024]{1,0:T(8,128)(2,1)S(1)}, bf16[64,1024]{1,0:T(8,128)(2,1)}, u32[]{:S(2)}) copy-start(bf16[64,1024]{1,0:T(8,128)(2,1)} %get-tuple-element.9.x_ref) | copy-start | bytes 393220
  27.1 0.9 %copy-start.2 = (bf16[64,1024]{1,0:T(8,128)(2,1)S(1)}, bf16[64,1024]{1,0:T(8,128)(2,1)}, u32[]{:S(2)}) copy-start(bf16[64,1024]{1,0:T(8,128)(2,1)} %get-tuple-element.10.dy_ref) | copy-start | bytes 393220
  28.0 0.9 %copy-start.3 = (bf16[64,1024]{1,0:T(8,128)(2,1)S(1)}, bf16[64,1024]{1,0:T(8,128)(2,1)}, u32[]{:S(2)}) copy-start(bf16[64,1024]{1,0:T(8,128)(2,1)} %get-tuple-element.8.back_ref) | copy-start | bytes 393220

commit v2 on v1

--- a/solution.py
+++ b/solution.py
@@ -11,6 +11,10 @@
 BF16 = jnp.bfloat16
 F32 = jnp.float32
 NT = (((1,), (1,)), ((), ()))
+
+
+def block_of(hidden_units):
+    return max(d for d in range(16, 177, 16) if hidden_units % d == 0)
 
 
 def bulk_wait(ref, count, sem):
@@ -28,10 +32,13 @@
     wg_hbm,
     wu_hbm,
     wd_hbm,
+    back_out,
+    gate_out,
+    up_out,
+    down_out,
     x_out,
     dy_out,
     dt_out,
-    back_out,
     tok,
     cot,
     wg,
@@ -173,6 +180,23 @@
     dt_out[0] = d_gate.T.astype(BF16)
     dt_out[1] = d_up.T.astype(BF16)
     dt_out[2] = hidden.T.astype(BF16)
+    lane_expert = lax.rem(lax.broadcasted_iota(jnp.int32, (1, rows), 1), experts)
+    hidden_units = wg.shape[1]
+    block = block_of(hidden_units)
+    for e in range(experts):
+        mine = jnp.where(lane_expert == e, 1.0, 0.0).astype(BF16)
+
+        def grads(i, carry):
+            at = pl.ds(pl.multiple_of(i * block, block), block)
+            for j, (out, other) in enumerate(
+                ((gate_out, x_out), (up_out, x_out), (down_out, dy_out))
+            ):
+                out[e, at, :] = jnp.dot(
+                    dt_out[j, at, :] * mine, other[...], preferred_element_type=F32
+                ).astype(BF16)
+            return carry
+
+        lax.fori_loop(0, hidden_units // block, grads, 0)
     bulk_wait(backbuf, n - 1, recv_sem.at[2])
     unpack(backbuf, back_out)
     bulk_wait(xbuf, n - 1, send_sem.at[0])
@@ -180,30 +204,47 @@
     bulk_wait(partmsg, n - 1, send_sem.at[2])
 
 
-def grads_kernel(
-    n_dp, experts, picks_ref, back_ref, x_ref, dy_ref, dt_ref, tokens_out, gate_out, up_out, down_out
+def store_kernel(
+    n_dp,
+    picks_ref,
+    back_hbm,
+    gate_in,
+    up_in,
+    down_in,
+    tokens_out,
+    gate_out,
+    up_out,
+    down_out,
+    back,
+    total,
+    sem,
 ):
-    expert = pl.program_id(0)
-
-    @pl.when((expert == 0) & (pl.program_id(1) == 0))
-    def _():
-        shape = (tokens_out.shape[0], picks_ref.shape[1])
-        chosen = jnp.where(
-            lax.broadcasted_iota(jnp.int32, shape, 0) == picks_ref[...], 1.0, 0.0
-        )
-        spread = jnp.concatenate([chosen] * n_dp, axis=1).astype(BF16)
-        tokens_out[...] = jnp.dot(
-            spread, back_ref[...], preferred_element_type=F32
-        ).astype(BF16)
-
-    rows = x_ref.shape[0]
-    lane = lax.broadcasted_iota(jnp.int32, (1, rows), 1)
-    mine = jnp.where(lax.rem(lane, experts) == expert, 1.0, 0.0).astype(BF16)
-    for i, (out, other) in enumerate(((gate_out, x_ref), (up_out, x_ref), (down_out, dy_ref))):
-        out[0] = jnp.dot(dt_ref[i] * mine, other[...], preferred_element_type=F32).astype(BF16)
+    load = pltpu.make_async_copy(back_hbm, back, sem.at[0])
+    load.start()
+    stores = [
+        pltpu.make_async_copy(src, dst, sem.at[1 + i])
+        for i, (src, dst) in enumerate(
+            ((gate_in, gate_out), (up_in, up_out), (down_in, down_out))
+        )
+    ]
+    for store in stores:
+        store.start()
+    shape = (total.shape[0], picks_ref.shape[1])
+    chosen = jnp.where(lax.broadcasted_iota(jnp.int32, shape, 0) == picks_ref[...], 1.0, 0.0)
+    spread = jnp.concatenate([chosen] * n_dp, axis=1).astype(BF16)
+    load.wait()
+    total[...] = jnp.dot(spread, back[...], preferred_element_type=F32).astype(BF16)
+    stores.append(pltpu.make_async_copy(total, tokens_out, sem.at[4]))
+    stores[-1].start()
+    for store in stores:
+        store.wait()
 
 
 def shards(n_dp, n_ex, tokens, cotangent, picks, gates, w_gate, w_up, w_down):
+    picks, gates, tokens, cotangent, w_gate, w_up, w_down = (
+        pltpu.with_memory_space_constraint(a, pltpu.HBM)
+        for a in (picks, gates, tokens, cotangent, w_gate, w_up, w_down)
+    )
     token_rows, width = tokens.shape
     experts, hidden, _ = w_gate.shape
     n = n_dp * n_ex
@@ -212,17 +253,15 @@
     weight = pltpu.VMEM((experts, hidden, width), BF16)
     vmem = pl.BlockSpec(memory_space=pltpu.VMEM)
     anywhere = pl.BlockSpec(memory_space=pl.ANY)
-    x, dy, dt, back = pl.pallas_call(
+    back, d_gate, d_up, d_down = pl.pallas_call(
         functools.partial(exchange_kernel, n_dp, n_ex),
-        out_shape=(
-            jax.ShapeDtypeStruct((rows, width), BF16),
-            jax.ShapeDtypeStruct((rows, width), BF16),
-            jax.ShapeDtypeStruct((3, hidden, rows), BF16),
-            jax.ShapeDtypeStruct((rows, width), BF16),
-        ),
+        out_shape=(pltpu.VMEM((rows, width), BF16),) + (weight,) * 3,
         in_specs=[vmem] * 2 + [anywhere] * 5,
         out_specs=(vmem,) * 4,
         scratch_shapes=[
+            pltpu.VMEM((rows, width), BF16),
+            pltpu.VMEM((rows, width), BF16),
+            pltpu.VMEM((3, hidden, rows), BF16),
             pltpu.VMEM((token_rows, width), BF16),
             pltpu.VMEM((token_rows, width), BF16),
             weight,
@@ -240,28 +279,23 @@
             pltpu.SemaphoreType.DMA((3,)),
         ],
         compiler_params=pltpu.CompilerParams(
-            collective_id=0, has_side_effects=True, vmem_limit_bytes=56 * 1024 * 1024
+            collective_id=0, has_side_effects=True, vmem_limit_bytes=28 * 1024 * 1024
         ),
     )(picks, gates, tokens, cotangent, w_gate, w_up, w_down)
 
-    step = max(d for d in range(16, 177, 16) if hidden % d == 0)
-    whole = lambda *shape: pl.BlockSpec(shape, lambda e, f: (0,) * len(shape))
-    tile = pl.BlockSpec((1, step, width), lambda e, f: (e, f, 0))
     grad = jax.ShapeDtypeStruct(w_gate.shape, BF16)
     return pl.pallas_call(
-        functools.partial(grads_kernel, n_dp, experts),
-        grid=(experts, hidden // step),
+        functools.partial(store_kernel, n_dp),
         out_shape=(jax.ShapeDtypeStruct(tokens.shape, BF16), grad, grad, grad),
-        in_specs=[
-            whole(*picks.shape),
-            whole(rows, width),
-            whole(rows, width),
-            whole(rows, width),
-            pl.BlockSpec((3, step, rows), lambda e, f: (0, f, 0)),
+        in_specs=[vmem] + [anywhere] * 4,
+        out_specs=(anywhere,) * 4,
+        scratch_shapes=[
+            pltpu.VMEM((rows, width), BF16),
+            pltpu.VMEM(tokens.shape, BF16),
+            pltpu.SemaphoreType.DMA((5,)),
         ],
-        out_specs=(whole(*tokens.shape), tile, tile, tile),
-        compiler_params=pltpu.CompilerParams(vmem_limit_bytes=48 * 1024 * 1024),
-    )(picks, back, x, dy, dt)
+        compiler_params=pltpu.CompilerParams(vmem_limit_bytes=8 * 1024 * 1024),
+    )(picks, back, d_gate, d_up, d_down)
 
 
 def solution(mesh):

time: 35.2 us -> 28.6 us (0.81)
  local copies, waits for them, and re-layouts: 3.76 us -> 0 us
  Pallas kernels: 30.5 us -> 27.8 us
    unnamed x10 -> x0, local copies, waits for them, and re-layouts: 3.76 us -> none
    pallas_call x1, Pallas kernels: 6.03 us -> 4.31 us  [shards(): pl.pallas_call(functools.partial(store_kernel, n_dp), out_shape=(jax.Shap...]
    pallas_call x1, Pallas kernels: 24.5 us -> 23.5 us  [shards(): pl.pallas_call(functools.partial(exchange_kernel, n_dp, n_ex), out_shape=...]
where the time goes in v2:
time: 28.6 us; the launch traced here: 28.4 us
  Pallas kernels  27.8 us (97%)
  between operations  0.64 us (2%)
    pallas_call x1, Pallas kernels, shards(): pl.pallas_call(functools.partial(exchange_kernel, n_dp, n_ex), out_shape=...  23.5 us
    pallas_call x1, Pallas kernels, shards(): pl.pallas_call(functools.partial(store_kernel, n_dp), out_shape=(jax.Shap...  4.31 us

profile of v2, /device:TPU:0, one launch (start us, length us, event | category | flops | bytes accessed | tf_op | source)
XLA Modules:
  0.0 28.4 jit_solution(1029638479618220048)
XLA Ops:
  0.6 23.5 %shard_map.102 = (bf16[64,1024]{1,0:T(8,128)(2,1)S(1)}, bf16[2,704,1024]{2,1,0:T(8,128)(2,1)S(1)}, bf16[2,704,1024]{2,1,0:T(8,128)(2,1)S(1)}, bf16[2,704,1024]{2,1,0:T(8,128)(2,1)S(1)}) custom-call(s32[1,16]{1,0:T(1,128)} %picks_ref.3, f32[1,16]{1,0:T(1,128)} %gates_ref.1, bf16[128,1024]{1,0:T(8,128)(2,1)} %tokens_hbm.1, bf16[128,1024]{1,0:T(8,128)(2,1)} %cot_hbm.1, ...), custom_call_target="tpu_custom_call" | custom-call | tf_op jit(solution)/shard_map/pallas_call | solution.py:256
  24.1 4.3 %shard_map.103 = (bf16[128,1024]{1,0:T(8,128)(2,1)}, bf16[2,704,1024]{2,1,0:T(8,128)(2,1)}, bf16[2,704,1024]{2,1,0:T(8,128)(2,1)}, bf16[2,704,1024]{2,1,0:T(8,128)(2,1)}) custom-call(s32[1,16]{1,0:T(1,128)} %picks_ref.3, bf16[64,1024]{1,0:T(8,128)(2,1)S(1)} %get-tuple-element.8.back_hbm, bf16[2,704,1024]{2,1,0:T(8,128)(2,1)S(1)} %get-tuple-element.9.gate_in, ...), custom_call_target="tpu_custom_call" | custom-call | tf_op jit(solution)/shard_map/pallas_call | solution.py:287

commit v3 on v2

v3 whole, which is shorter than its diff:
```python
import functools

import jax
import jax.numpy as jnp
from jax import lax
from jax.experimental import pallas as pl
from jax.experimental.pallas import tpu as pltpu
from jax.sharding import PartitionSpec as P

LANES = 128
BF16 = jnp.bfloat16
F32 = jnp.float32
NT = (((1,), (1,)), ((), ()))


def block_of(hidden_units):
    return max(d for d in range(16, 177, 16) if hidden_units % d == 0)


def bulk_wait(ref, count, sem):
    part = ref.at[pl.ds(0, count)]
    pltpu.make_async_copy(part, part, sem).wait()


def exchange_kernel(
    n_dp,
    n_ex,
    picks_ref,
    gates_ref,
    tokens_hbm,
    cot_hbm,
    wg_hbm,
    wu_hbm,
    wd_hbm,
    back_out,
    gate_out,
    up_out,
    down_out,
    x_out,
    dy_out,
    dt_out,
    tok,
    cot,
    wg,
    wu,
    wd,
    wide,
    xmsg,
    dymsg,
    xbuf,
    dybuf,
    partmsg,
    backbuf,
    load_sem,
    send_sem,
    recv_sem,
):
    n = n_dp * n_ex
    experts, _, width = wg.shape
    chunks = width // LANES
    picked = picks_ref.shape[1]
    token_rows = tok.shape[0]
    my_dp, my_ex = lax.axis_index("dp"), lax.axis_index("expert")
    me = my_dp * n_ex + my_ex

    loads = [
        pltpu.make_async_copy(src, dst, load_sem.at[i])
        for i, (src, dst) in enumerate(
            ((tokens_hbm, tok), (cot_hbm, cot), (wg_hbm, wg), (wu_hbm, wu), (wd_hbm, wd))
        )
    ]
    for load in loads:
        load.start()

    def wrap(value, size):
        return jnp.where(value >= size, value - size, value)

    experts_at = [wrap(my_ex + b, n_ex) for b in range(n_ex)]

    def each_peer(act):
        for b in range(1, n_ex):
            act(my_dp, experts_at[b])

        def ring(a, carry):
            at_dp = wrap(my_dp + a, n_dp)
            for b in range(n_ex):
                act(at_dp, experts_at[b])
            return carry

        lax.fori_loop(1, n_dp, ring, 0)

    barrier = pltpu.get_barrier_semaphore()

    def greet(dp, ex):
        pl.semaphore_signal(
            barrier, inc=1, device_id=(dp, ex), device_id_type=pl.DeviceIdType.MESH
        )

    each_peer(greet)

    eye = lax.broadcasted_iota(jnp.int32, (picked, picked), 0) == lax.broadcasted_iota(
        jnp.int32, (picked, picked), 1
    )
    pick_col = jnp.sum(
        jnp.where(eye, picks_ref[...].astype(F32), 0.0), axis=1, keepdims=True
    ).astype(jnp.int32)
    gate_col = jnp.sum(jnp.where(eye, gates_ref[...], 0.0), axis=1, keepdims=True)
    selector = jnp.where(
        lax.broadcasted_iota(jnp.int32, (picked, token_rows), 1) == pick_col, 1.0, 0.0
    ).astype(BF16)

    def pack(parts, msg):
        count = parts[0].shape[0]
        stride = len(parts) * chunks
        for e, value in enumerate(parts):
            for k in range(chunks):
                wide[pl.ds(e * chunks + k, count, stride=stride), :] = value[
                    :, k * LANES : (k + 1) * LANES
                ]
        msg[...] = wide[pl.ds(0, count * stride), :].astype(BF16).reshape(msg.shape)

    def unpack(buf, out):
        wide[...] = buf[...].reshape(wide.shape).astype(F32)
        for e in range(experts):
            for k in range(chunks):
                out[e, :, k * LANES : (k + 1) * LANES] = wide[
                    pl.ds(e * chunks + k, n, stride=experts * chunks), :
                ].astype(BF16)

    def send_all(msg, buf, slot, by_expert):
        def one(dp, ex):
            pltpu.make_async_remote_copy(
                src_ref=msg.at[ex if by_expert else dp * n_ex + ex],
                dst_ref=buf.at[me],
                send_sem=send_sem.at[slot],
                recv_sem=recv_sem.at[slot],
                device_id=(dp, ex),
                device_id_type=pl.DeviceIdType.MESH,
            ).start()

        each_peer(one)
        buf[me] = msg[my_ex if by_expert else me]

    loads[0].wait()
    pack([jnp.dot(selector, tok[...], preferred_element_type=F32)], xmsg)
    pl.semaphore_wait(barrier, n - 1)
    send_all(xmsg, xbuf, 0, True)
    loads[1].wait()
    pack([jnp.dot(selector, cot[...], preferred_element_type=F32) * gate_col], dymsg)
    send_all(dymsg, dybuf, 1, True)

    def forward(e, value, weights):
        return lax.dot_general(value[e], weights[e], NT, preferred_element_type=F32)

    every = range(experts)
    bulk_wait(xbuf, n - 1, recv_sem.at[0])
    unpack(xbuf, x_out)
    loads[2].wait()
    pre_gate = [forward(e, x_out, wg) for e in every]
    loads[3].wait()
    pre_up = [forward(e, x_out, wu) for e in every]
    sigmoid_g = [jax.nn.sigmoid(g) for g in pre_gate]
    active = [g * s for g, s in zip(pre_gate, sigmoid_g)]
    slope = [
        u * s * (1.0 + g * (1.0 - s)) for g, u, s in zip(pre_gate, pre_up, sigmoid_g)
    ]
    for e in every:
        dt_out[e, 2] = (active[e] * pre_up[e]).T.astype(BF16)
    loads[4].wait()
    bulk_wait(dybuf, n - 1, recv_sem.at[1])
    unpack(dybuf, dy_out)
    grad_hidden = [forward(e, dy_out, wd) for e in every]
    d_up = [h * a for h, a in zip(grad_hidden, active)]
    d_gate = [h * s for h, s in zip(grad_hidden, slope)]
    pack(
        [
            jnp.dot(d_gate[e].astype(BF16), wg[e], preferred_element_type=F32)
            + jnp.dot(d_up[e].astype(BF16), wu[e], preferred_element_type=F32)
            for e in every
        ],
        partmsg,
    )
    send_all(partmsg, backbuf, 2, False)
    hidden_units = wg.shape[1]
    block = block_of(hidden_units)
    for e in every:
        dt_out[e, 0] = d_gate[e].T.astype(BF16)
        dt_out[e, 1] = d_up[e].T.astype(BF16)

        def grads(i, carry):
            at = pl.ds(pl.multiple_of(i * block, block), block)
            for j, (out, other) in enumerate(
                ((gate_out, x_out), (up_out, x_out), (down_out, dy_out))
            ):
                out[e, at, :] = jnp.dot(
                    dt_out[e, j, at, :], other[e], preferred_element_type=F32
                ).astype(BF16)
            return carry

        lax.fori_loop(0, hidden_units // block, grads, 0)
    bulk_wait(backbuf, n - 1, recv_sem.at[2])
    unpack(backbuf, back_out)
    bulk_wait(xbuf, n - 1, send_sem.at[0])
    bulk_wait(dybuf, n - 1, send_sem.at[1])
    bulk_wait(partmsg, n - 1, send_sem.at[2])


def store_kernel(
    n_dp,
    n_ex,
    picks_ref,
    back_hbm,
    gate_in,
    up_in,
    down_in,
    tokens_out,
    gate_out,
    up_out,
    down_out,
    back,
    total,
    sem,
    store_sem,
):
    load = pltpu.make_async_copy(back_hbm, back, sem.at[0])
    load.start()
    experts, hidden_units, _ = gate_in.shape
    half = hidden_units // 2 // 16 * 16
    stores = []
    for e in range(experts):
        for src, dst in ((gate_in, gate_out), (up_in, up_out), (down_in, down_out)):
            for at in (pl.ds(0, half), pl.ds(half, hidden_units - half)):
                stores.append(
                    pltpu.make_async_copy(
                        src.at[e, at], dst.at[e, at], store_sem.at[len(stores)]
                    )
                )
                stores[-1].start()
    token_rows = total.shape[0]
    picks = picks_ref[...].astype(F32)
    load.wait()
    columns = lax.broadcasted_iota(jnp.int32, (picks.shape[1], n_dp * n_ex), 0)
    places = lax.broadcasted_iota(jnp.int32, (picks.shape[1], n_dp * n_ex), 1)
    summed = jnp.zeros(total.shape, F32)
    for e in range(experts):
        wanted = jnp.where(columns == lax.rem(places, n_ex) * experts + e, 1.0, 0.0)
        row = jnp.dot(
            jnp.broadcast_to(picks, (8, picks.shape[1])).astype(BF16),
            wanted.astype(BF16),
            preferred_element_type=F32,
        )[:1]
        chosen = jnp.where(
            lax.broadcasted_iota(jnp.int32, (token_rows, n_dp * n_ex), 0).astype(F32) == row,
            1.0,
            0.0,
        ).astype(BF16)
        summed += jnp.dot(chosen, back[e], preferred_element_type=F32)
    total[...] = summed.astype(BF16)
    stores.append(pltpu.make_async_copy(total, tokens_out, sem.at[1]))
    stores[-1].start()
    for store in stores:
        store.wait()


def shards(n_dp, n_ex, tokens, cotangent, picks, gates, w_gate, w_up, w_down):
    picks, gates, tokens, cotangent, w_gate, w_up, w_down = (
        pltpu.with_memory_space_constraint(a, pltpu.HBM)
        for a in (picks, gates, tokens, cotangent, w_gate, w_up, w_down)
    )
    token_rows, width = tokens.shape
    experts, hidden, _ = w_gate.shape
    n = n_dp * n_ex
    rows = (experts, n, width)
    message = (experts * width // LANES, LANES)
    weight = pltpu.VMEM((experts, hidden, width), BF16)
    vmem = pl.BlockSpec(memory_space=pltpu.VMEM)
    anywhere = pl.BlockSpec(memory_space=pl.ANY)
    back, d_gate, d_up, d_down = pl.pallas_call(
        functools.partial(exchange_kernel, n_dp, n_ex),
        out_shape=(pltpu.VMEM(rows, BF16),) + (weight,) * 3,
        in_specs=[vmem] * 2 + [anywhere] * 5,
        out_specs=(vmem,) * 4,
        scratch_shapes=[
            pltpu.VMEM(rows, BF16),
            pltpu.VMEM(rows, BF16),
            pltpu.VMEM((experts, 3, hidden, n), BF16),
            pltpu.VMEM((token_rows, width), BF16),
            pltpu.VMEM((token_rows, width), BF16),
            weight,
            weight,
            weight,
            pltpu.VMEM((n * experts * width // LANES, LANES), F32),
            pltpu.VMEM((n_ex,) + message, BF16),
            pltpu.VMEM((n_ex,) + message, BF16),
            pltpu.VMEM((n,) + message, BF16),
            pltpu.VMEM((n,) + message, BF16),
            pltpu.VMEM((n,) + message, BF16),
            pltpu.VMEM((n,) + message, BF16),
            pltpu.SemaphoreType.DMA((5,)),
            pltpu.SemaphoreType.DMA((3,)),
            pltpu.SemaphoreType.DMA((3,)),
        ],
        compiler_params=pltpu.CompilerParams(
            collective_id=0, has_side_effects=True, vmem_limit_bytes=28 * 1024 * 1024
        ),
    )(picks, gates, tokens, cotangent, w_gate, w_up, w_down)

    grad = jax.ShapeDtypeStruct(w_gate.shape, BF16)
    return pl.pallas_call(
        functools.partial(store_kernel, n_dp, n_ex),
        out_shape=(jax.ShapeDtypeStruct(tokens.shape, BF16), grad, grad, grad),
        in_specs=[vmem] + [anywhere] * 4,
        out_specs=(anywhere,) * 4,
        scratch_shapes=[
            pltpu.VMEM(rows, BF16),
            pltpu.VMEM(tokens.shape, BF16),
            pltpu.SemaphoreType.DMA((2,)),
            pltpu.SemaphoreType.DMA((6 * experts,)),
        ],
        compiler_params=pltpu.CompilerParams(vmem_limit_bytes=8 * 1024 * 1024),
    )(picks, back, d_gate, d_up, d_down)


def solution(mesh):
    spread = P(("dp", "expert"), None)
    weight = P("expert", "dp", None)
    return jax.shard_map(
        functools.partial(shards, mesh.shape["dp"], mesh.shape["expert"]),
        mesh=mesh,
        in_specs=(spread,) * 4 + (weight,) * 3,
        out_specs=(spread,) + (weight,) * 3,
        check_vma=False,
    )
```

time: 28.6 us -> 28.8 us (level)
  no operation moved by 1% of the time
where the time goes in v3:
time: 28.8 us; the launch traced here: 28.7 us
  Pallas kernels  28 us (97%)
  between operations  0.64 us (2%)
    pallas_call x1, Pallas kernels, shards(): pl.pallas_call(functools.partial(exchange_kernel, n_dp, n_ex), out_shape=...  23.7 us
    pallas_call x1, Pallas kernels, shards(): pl.pallas_call(functools.partial(store_kernel, n_dp, n_ex), out_shape=(ja...  4.33 us

profile of v3, /device:TPU:0, one launch (start us, length us, event | category | flops | bytes accessed | tf_op | source)
XLA Modules:
  0.0 28.7 jit_solution(8177602195488054376)
XLA Ops:
  0.6 23.7 %shard_map.102 = (bf16[2,32,1024]{2,1,0:T(8,128)(2,1)S(1)}, bf16[2,704,1024]{2,1,0:T(8,128)(2,1)S(1)}, bf16[2,704,1024]{2,1,0:T(8,128)(2,1)S(1)}, bf16[2,704,1024]{2,1,0:T(8,128)(2,1)S(1)}) custom-call(s32[1,16]{1,0:T(1,128)} %picks_ref.3, f32[1,16]{1,0:T(1,128)} %gates_ref.1, bf16[128,1024]{1,0:T(8,128)(2,1)} %tokens_hbm.1, bf16[128,1024]{1,0:T(8,128)(2,1)} %cot_hbm.1, ...), custom_call_target="tpu_custom_call" | custom-call | tf_op jit(solution)/shard_map/pallas_call | solution.py:278
  24.3 4.3 %shard_map.103 = (bf16[128,1024]{1,0:T(8,128)(2,1)}, bf16[2,704,1024]{2,1,0:T(8,128)(2,1)}, bf16[2,704,1024]{2,1,0:T(8,128)(2,1)}, bf16[2,704,1024]{2,1,0:T(8,128)(2,1)}) custom-call(s32[1,16]{1,0:T(1,128)} %picks_ref.3, bf16[2,32,1024]{2,1,0:T(8,128)(2,1)S(1)} %get-tuple-element.8.back_hbm, bf16[2,704,1024]{2,1,0:T(8,128)(2,1)S(1)} %get-tuple-element.9.gate_in, ...), custom_call_target="tpu_custom_call" | custom-call | tf_op jit(solution)/shard_map/pallas_call | solution.py:309

commit v4 on v3

--- a/solution.py
+++ b/solution.py
@@ -61,7 +61,11 @@
     picked = picks_ref.shape[1]
     token_rows = tok.shape[0]
     my_dp, my_ex = lax.axis_index("dp"), lax.axis_index("expert")
-    me = my_dp * n_ex + my_ex
+    cores = 2
+    n_chip = n // cores
+    my_core, my_half = lax.rem(my_dp, cores), my_dp // cores
+    my_chip = my_half * n_ex + my_ex
+    me = my_core * n_chip + my_chip
 
     loads = [
         pltpu.make_async_copy(src, dst, load_sem.at[i])
@@ -77,26 +81,33 @@
 
     experts_at = [wrap(my_ex + b, n_ex) for b in range(n_ex)]
 
-    def each_peer(act):
+    def each_chip(act):
         for b in range(1, n_ex):
-            act(my_dp, experts_at[b])
+            act(my_half, experts_at[b])
 
         def ring(a, carry):
-            at_dp = wrap(my_dp + a, n_dp)
+            half = wrap(my_half + a, n_dp // cores)
             for b in range(n_ex):
-                act(at_dp, experts_at[b])
+                act(half, experts_at[b])
             return carry
 
-        lax.fori_loop(1, n_dp, ring, 0)
+        lax.fori_loop(1, n_dp // cores, ring, 0)
+
+    sibling = (my_half * cores + 1 - my_core, my_ex)
 
     barrier = pltpu.get_barrier_semaphore()
 
-    def greet(dp, ex):
+    def greet(where):
         pl.semaphore_signal(
-            barrier, inc=1, device_id=(dp, ex), device_id_type=pl.DeviceIdType.MESH
+            barrier, inc=1, device_id=where, device_id_type=pl.DeviceIdType.MESH
         )
 
-    each_peer(greet)
+    def greet_chip(half, ex):
+        for core in range(cores):
+            greet((half * cores + core, ex))
+
+    greet(sibling)
+    each_chip(greet_chip)
 
     eye = lax.broadcasted_iota(jnp.int32, (picked, picked), 0) == lax.broadcasted_iota(
         jnp.int32, (picked, picked), 1
@@ -127,37 +138,59 @@
                     pl.ds(e * chunks + k, n, stride=experts * chunks), :
                 ].astype(BF16)
 
-    def send_all(msg, buf, slot, by_expert):
-        def one(dp, ex):
-            pltpu.make_async_remote_copy(
-                src_ref=msg.at[ex if by_expert else dp * n_ex + ex],
-                dst_ref=buf.at[me],
-                send_sem=send_sem.at[slot],
-                recv_sem=recv_sem.at[slot],
-                device_id=(dp, ex),
-                device_id_type=pl.DeviceIdType.MESH,
-            ).start()
-
-        each_peer(one)
-        buf[me] = msg[my_ex if by_expert else me]
+    def remote(src, dst, slot, where):
+        return pltpu.make_async_remote_copy(
+            src_ref=src,
+            dst_ref=dst,
+            send_sem=send_sem.at[slot],
+            recv_sem=recv_sem.at[slot],
+            device_id=where,
+            device_id_type=pl.DeviceIdType.MESH,
+        )
+
+    def send_chips(msg, buf, slot):
+        def one(half, ex):
+            where = (half * cores + my_core, ex)
+            remote(msg.at[ex], buf.at[my_core, my_chip], slot, where).start()
+
+        each_chip(one)
+        buf[my_core, my_chip] = msg[my_ex]
+
+    def hand_over(buf, slot):
+        bulk_wait(buf.at[0], n_chip - 1, recv_sem.at[slot])
+        copy = remote(buf.at[my_core], buf.at[my_core], slot + 1, sibling)
+        copy.start()
+        return copy
+
+    def send_back(msg, buf, slot):
+        def one(half, ex):
+            for core in range(cores):
+                spot = core * n_chip + half * n_ex + ex
+                remote(msg.at[spot], buf.at[me], slot, (half * cores + core, ex)).start()
+
+        each_chip(one)
+        remote(msg.at[(1 - my_core) * n_chip + my_chip], buf.at[me], slot, sibling).start()
+        buf[me] = msg[me]
 
     loads[0].wait()
     pack([jnp.dot(selector, tok[...], preferred_element_type=F32)], xmsg)
     pl.semaphore_wait(barrier, n - 1)
-    send_all(xmsg, xbuf, 0, True)
+    send_chips(xmsg, xbuf, 0)
     loads[1].wait()
     pack([jnp.dot(selector, cot[...], preferred_element_type=F32) * gate_col], dymsg)
-    send_all(dymsg, dybuf, 1, True)
+    send_chips(dymsg, dybuf, 2)
 
     def forward(e, value, weights):
         return lax.dot_general(value[e], weights[e], NT, preferred_element_type=F32)
 
     every = range(experts)
-    bulk_wait(xbuf, n - 1, recv_sem.at[0])
+    x_copy = hand_over(xbuf, 0)
+    x_copy.wait()
     unpack(xbuf, x_out)
     loads[2].wait()
     pre_gate = [forward(e, x_out, wg) for e in every]
     loads[3].wait()
+    dy_copy = hand_over(dybuf, 2)
     pre_up = [forward(e, x_out, wu) for e in every]
     sigmoid_g = [jax.nn.sigmoid(g) for g in pre_gate]
     active = [g * s for g, s in zip(pre_gate, sigmoid_g)]
@@ -167,7 +200,7 @@
     for e in every:
         dt_out[e, 2] = (active[e] * pre_up[e]).T.astype(BF16)
     loads[4].wait()
-    bulk_wait(dybuf, n - 1, recv_sem.at[1])
+    dy_copy.wait()
     unpack(dybuf, dy_out)
     grad_hidden = [forward(e, dy_out, wd) for e in every]
     d_up = [h * a for h, a in zip(grad_hidden, active)]
@@ -180,7 +213,7 @@
         ],
         partmsg,
     )
-    send_all(partmsg, backbuf, 2, False)
+    send_back(partmsg, backbuf, 4)
     hidden_units = wg.shape[1]
     block = block_of(hidden_units)
     for e in every:
@@ -198,11 +231,11 @@
             return carry
 
         lax.fori_loop(0, hidden_units // block, grads, 0)
-    bulk_wait(backbuf, n - 1, recv_sem.at[2])
+    bulk_wait(backbuf, n - 1, recv_sem.at[4])
     unpack(backbuf, back_out)
-    bulk_wait(xbuf, n - 1, send_sem.at[0])
-    bulk_wait(dybuf, n - 1, send_sem.at[1])
-    bulk_wait(partmsg, n - 1, send_sem.at[2])
+    bulk_wait(xbuf.at[0], n_chip - 1, send_sem.at[0])
+    bulk_wait(dybuf.at[0], n_chip - 1, send_sem.at[2])
+    bulk_wait(partmsg, n - 1, send_sem.at[4])
 
 
 def store_kernel(
@@ -292,13 +325,13 @@
             pltpu.VMEM((n * experts * width // LANES, LANES), F32),
             pltpu.VMEM((n_ex,) + message, BF16),
             pltpu.VMEM((n_ex,) + message, BF16),
-            pltpu.VMEM((n,) + message, BF16),
-            pltpu.VMEM((n,) + message, BF16),
+            pltpu.VMEM((2, n // 2) + message, BF16),
+            pltpu.VMEM((2, n // 2) + message, BF16),
             pltpu.VMEM((n,) + message, BF16),
             pltpu.VMEM((n,) + message, BF16),
             pltpu.SemaphoreType.DMA((5,)),
-            pltpu.SemaphoreType.DMA((3,)),
-            pltpu.SemaphoreType.DMA((3,)),
+            pltpu.SemaphoreType.DMA((5,)),
+            pltpu.SemaphoreType.DMA((5,)),
         ],
         compiler_params=pltpu.CompilerParams(
             collective_id=0, has_side_effects=True, vmem_limit_bytes=28 * 1024 * 1024

time: 28.8 us -> 28.8 us (level)
  no operation moved by 1% of the time
where the time goes in v4:
time: 28.8 us; the launch traced here: 28.7 us
  Pallas kernels  28 us (97%)
  between operations  0.64 us (2%)
    pallas_call x1, Pallas kernels, shards(): pl.pallas_call(functools.partial(exchange_kernel, n_dp, n_ex), out_shape=...  23.7 us
    pallas_call x1, Pallas kernels, shards(): pl.pallas_call(functools.partial(store_kernel, n_dp, n_ex), out_shape=(ja...  4.33 us

profile of v4, /device:TPU:0, one launch (start us, length us, event | category | flops | bytes accessed | tf_op | source)
XLA Modules:
  0.0 28.7 jit_solution(5883893320558105514)
XLA Ops:
  0.6 23.7 %shard_map.102 = (bf16[2,32,1024]{2,1,0:T(8,128)(2,1)S(1)}, bf16[2,704,1024]{2,1,0:T(8,128)(2,1)S(1)}, bf16[2,704,1024]{2,1,0:T(8,128)(2,1)S(1)}, bf16[2,704,1024]{2,1,0:T(8,128)(2,1)S(1)}) custom-call(s32[1,16]{1,0:T(1,128)} %picks_ref.3, f32[1,16]{1,0:T(1,128)} %gates_ref.1, bf16[128,1024]{1,0:T(8,128)(2,1)} %tokens_hbm.1, bf16[128,1024]{1,0:T(8,128)(2,1)} %cot_hbm.1, ...), custom_call_target="tpu_custom_call" | custom-call | tf_op jit(solution)/shard_map/pallas_call | solution.py:311
  24.3 4.3 %shard_map.103 = (bf16[128,1024]{1,0:T(8,128)(2,1)}, bf16[2,704,1024]{2,1,0:T(8,128)(2,1)}, bf16[2,704,1024]{2,1,0:T(8,128)(2,1)}, bf16[2,704,1024]{2,1,0:T(8,128)(2,1)}) custom-call(s32[1,16]{1,0:T(1,128)} %picks_ref.3, bf16[2,32,1024]{2,1,0:T(8,128)(2,1)S(1)} %get-tuple-element.8.back_hbm, bf16[2,704,1024]{2,1,0:T(8,128)(2,1)S(1)} %get-tuple-element.9.gate_in, ...), custom_call_target="tpu_custom_call" | custom-call | tf_op jit(solution)/shard_map/pallas_call | solution.py:342

commit v5 on v4

--- a/solution.py
+++ b/solution.py
@@ -181,7 +181,7 @@
     send_chips(dymsg, dybuf, 2)
 
     def forward(e, value, weights):
-        return lax.dot_general(value[e], weights[e], NT, preferred_element_type=F32)
+        return lax.dot_general(weights[e], value[e], NT, preferred_element_type=F32).T
 
     every = range(experts)
     x_copy = hand_over(xbuf, 0)

time: 28.8 us -> 29 us (level)
  no operation moved by 1% of the time
where the time goes in v5:
time: 29 us; the launch traced here: 28.9 us
  Pallas kernels  28.2 us (97%)
  between operations  0.64 us (2%)
    pallas_call x1, Pallas kernels, shards(): pl.pallas_call(functools.partial(exchange_kernel, n_dp, n_ex), out_shape=...  23.9 us
    pallas_call x1, Pallas kernels, shards(): pl.pallas_call(functools.partial(store_kernel, n_dp, n_ex), out_shape=(ja...  4.33 us

profile of v5, /device:TPU:0, one launch (start us, length us, event | category | flops | bytes accessed | tf_op | source)
XLA Modules:
  0.0 28.9 jit_solution(14930216272465070516)
XLA Ops:
  0.6 23.9 %shard_map.102 = (bf16[2,32,1024]{2,1,0:T(8,128)(2,1)S(1)}, bf16[2,704,1024]{2,1,0:T(8,128)(2,1)S(1)}, bf16[2,704,1024]{2,1,0:T(8,128)(2,1)S(1)}, bf16[2,704,1024]{2,1,0:T(8,128)(2,1)S(1)}) custom-call(s32[1,16]{1,0:T(1,128)} %picks_ref.3, f32[1,16]{1,0:T(1,128)} %gates_ref.1, bf16[128,1024]{1,0:T(8,128)(2,1)} %tokens_hbm.1, bf16[128,1024]{1,0:T(8,128)(2,1)} %cot_hbm.1, ...), custom_call_target="tpu_custom_call" | custom-call | tf_op jit(solution)/shard_map/pallas_call | solution.py:311
  24.5 4.3 %shard_map.103 = (bf16[128,1024]{1,0:T(8,128)(2,1)}, bf16[2,704,1024]{2,1,0:T(8,128)(2,1)}, bf16[2,704,1024]{2,1,0:T(8,128)(2,1)}, bf16[2,704,1024]{2,1,0:T(8,128)(2,1)}) custom-call(s32[1,16]{1,0:T(1,128)} %picks_ref.3, bf16[2,32,1024]{2,1,0:T(8,128)(2,1)S(1)} %get-tuple-element.8.back_hbm, bf16[2,704,1024]{2,1,0:T(8,128)(2,1)S(1)} %get-tuple-element.9.gate_in, ...), custom_call_target="tpu_custom_call" | custom-call | tf_op jit(solution)/shard_map/pallas_call | solution.py:342

commit v6 on v4

--- a/solution.py
+++ b/solution.py
@@ -22,11 +22,22 @@
     pltpu.make_async_copy(part, part, sem).wait()
 
 
+def unpack(buf, wide, out):
+    experts, n, width = out.shape
+    chunks = width // LANES
+    wide[...] = buf[...].reshape(wide.shape).astype(F32)
+    for e in range(experts):
+        for k in range(chunks):
+            out[e, :, k * LANES : (k + 1) * LANES] = wide[
+                pl.ds(e * chunks + k, n, stride=experts * chunks), :
+            ].astype(BF16)
+
+
 def exchange_kernel(
     n_dp,
     n_ex,
-    picks_ref,
-    gates_ref,
+    picks_hbm,
+    gates_hbm,
     tokens_hbm,
     cot_hbm,
     wg_hbm,
@@ -39,6 +50,8 @@
     x_out,
     dy_out,
     dt_out,
+    picks_ref,
+    gates_ref,
     tok,
     cot,
     wg,
@@ -70,7 +83,15 @@
     loads = [
         pltpu.make_async_copy(src, dst, load_sem.at[i])
         for i, (src, dst) in enumerate(
-            ((tokens_hbm, tok), (cot_hbm, cot), (wg_hbm, wg), (wu_hbm, wu), (wd_hbm, wd))
+            (
+                (picks_hbm, picks_ref),
+                (tokens_hbm, tok),
+                (gates_hbm, gates_ref),
+                (cot_hbm, cot),
+                (wg_hbm, wg),
+                (wu_hbm, wu),
+                (wd_hbm, wd),
+            )
         )
     ]
     for load in loads:
@@ -112,10 +133,10 @@
     eye = lax.broadcasted_iota(jnp.int32, (picked, picked), 0) == lax.broadcasted_iota(
         jnp.int32, (picked, picked), 1
     )
+    loads[0].wait()
     pick_col = jnp.sum(
         jnp.where(eye, picks_ref[...].astype(F32), 0.0), axis=1, keepdims=True
     ).astype(jnp.int32)
-    gate_col = jnp.sum(jnp.where(eye, gates_ref[...], 0.0), axis=1, keepdims=True)
     selector = jnp.where(
         lax.broadcasted_iota(jnp.int32, (picked, token_rows), 1) == pick_col, 1.0, 0.0
     ).astype(BF16)
@@ -130,14 +151,6 @@
                 ]
         msg[...] = wide[pl.ds(0, count * stride), :].astype(BF16).reshape(msg.shape)
 
-    def unpack(buf, out):
-        wide[...] = buf[...].reshape(wide.shape).astype(F32)
-        for e in range(experts):
-            for k in range(chunks):
-                out[e, :, k * LANES : (k + 1) * LANES] = wide[
-                    pl.ds(e * chunks + k, n, stride=experts * chunks), :
-                ].astype(BF16)
-
     def remote(src, dst, slot, where):
         return pltpu.make_async_remote_copy(
             src_ref=src,
@@ -172,11 +185,13 @@
         remote(msg.at[(1 - my_core) * n_chip + my_chip], buf.at[me], slot, sibling).start()
         buf[me] = msg[me]
 
-    loads[0].wait()
+    loads[1].wait()
     pack([jnp.dot(selector, tok[...], preferred_element_type=F32)], xmsg)
     pl.semaphore_wait(barrier, n - 1)
     send_chips(xmsg, xbuf, 0)
-    loads[1].wait()
+    loads[2].wait()
+    gate_col = jnp.sum(jnp.where(eye, gates_ref[...], 0.0), axis=1, keepdims=True)
+    loads[3].wait()
     pack([jnp.dot(selector, cot[...], preferred_element_type=F32) * gate_col], dymsg)
     send_chips(dymsg, dybuf, 2)
 
@@ -186,10 +201,10 @@
     every = range(experts)
     x_copy = hand_over(xbuf, 0)
     x_copy.wait()
-    unpack(xbuf, x_out)
-    loads[2].wait()
+    unpack(xbuf, wide, x_out)
+    loads[4].wait()
     pre_gate = [forward(e, x_out, wg) for e in every]
-    loads[3].wait()
+    loads[5].wait()
     dy_copy = hand_over(dybuf, 2)
     pre_up = [forward(e, x_out, wu) for e in every]
     sigmoid_g = [jax.nn.sigmoid(g) for g in pre_gate]
@@ -197,11 +212,10 @@
     slope = [
         u * s * (1.0 + g * (1.0 - s)) for g, u, s in zip(pre_gate, pre_up, sigmoid_g)
     ]
-    for e in every:
-        dt_out[e, 2] = (active[e] * pre_up[e]).T.astype(BF16)
-    loads[4].wait()
+    hidden = [a * u for a, u in zip(active, pre_up)]
+    loads[6].wait()
     dy_copy.wait()
-    unpack(dybuf, dy_out)
+    unpack(dybuf, wide, dy_out)
     grad_hidden = [forward(e, dy_out, wd) for e in every]
     d_up = [h * a for h, a in zip(grad_hidden, active)]
     d_gate = [h * s for h, s in zip(grad_hidden, slope)]
@@ -219,6 +233,7 @@
     for e in every:
         dt_out[e, 0] = d_gate[e].T.astype(BF16)
         dt_out[e, 1] = d_up[e].T.astype(BF16)
+        dt_out[e, 2] = hidden[e].T.astype(BF16)
 
         def grads(i, carry):
             at = pl.ds(pl.multiple_of(i * block, block), block)
@@ -232,7 +247,7 @@
 
         lax.fori_loop(0, hidden_units // block, grads, 0)
     bulk_wait(backbuf, n - 1, recv_sem.at[4])
-    unpack(backbuf, back_out)
+    back_out[...] = backbuf[...]
     bulk_wait(xbuf.at[0], n_chip - 1, send_sem.at[0])
     bulk_wait(dybuf.at[0], n_chip - 1, send_sem.at[2])
     bulk_wait(partmsg, n - 1, send_sem.at[4])
@@ -241,8 +256,8 @@
 def store_kernel(
     n_dp,
     n_ex,
-    picks_ref,
-    back_hbm,
+    picks_hbm,
+    back_in,
     gate_in,
     up_in,
     down_in,
@@ -250,12 +265,17 @@
     gate_out,
     up_out,
     down_out,
+    picks_ref,
+    raw,
+    wide,
     back,
     total,
     sem,
     store_sem,
 ):
-    load = pltpu.make_async_copy(back_hbm, back, sem.at[0])
+    picks_load = pltpu.make_async_copy(picks_hbm, picks_ref, sem.at[0])
+    picks_load.start()
+    load = pltpu.make_async_copy(back_in, raw, sem.at[2])
     load.start()
     experts, hidden_units, _ = gate_in.shape
     half = hidden_units // 2 // 16 * 16
@@ -270,8 +290,10 @@
                 )
                 stores[-1].start()
     token_rows = total.shape[0]
+    load.wait()
+    unpack(raw, wide, back)
+    picks_load.wait()
     picks = picks_ref[...].astype(F32)
-    load.wait()
     columns = lax.broadcasted_iota(jnp.int32, (picks.shape[1], n_dp * n_ex), 0)
     places = lax.broadcasted_iota(jnp.int32, (picks.shape[1], n_dp * n_ex), 1)
     summed = jnp.zeros(total.shape, F32)
@@ -310,13 +332,15 @@
     anywhere = pl.BlockSpec(memory_space=pl.ANY)
     back, d_gate, d_up, d_down = pl.pallas_call(
         functools.partial(exchange_kernel, n_dp, n_ex),
-        out_shape=(pltpu.VMEM(rows, BF16),) + (weight,) * 3,
-        in_specs=[vmem] * 2 + [anywhere] * 5,
+        out_shape=(pltpu.VMEM((n,) + message, BF16),) + (weight,) * 3,
+        in_specs=[anywhere] * 7,
         out_specs=(vmem,) * 4,
         scratch_shapes=[
             pltpu.VMEM(rows, BF16),
             pltpu.VMEM(rows, BF16),
             pltpu.VMEM((experts, 3, hidden, n), BF16),
+            pltpu.VMEM(picks.shape, jnp.int32),
+            pltpu.VMEM(gates.shape, F32),
             pltpu.VMEM((token_rows, width), BF16),
             pltpu.VMEM((token_rows, width), BF16),
             weight,
@@ -329,7 +353,7 @@
             pltpu.VMEM((2, n // 2) + message, BF16),
             pltpu.VMEM((n,) + message, BF16),
             pltpu.VMEM((n,) + message, BF16),
-            pltpu.SemaphoreType.DMA((5,)),
+            pltpu.SemaphoreType.DMA((7,)),
             pltpu.SemaphoreType.DMA((5,)),
             pltpu.SemaphoreType.DMA((5,)),
         ],
@@ -342,15 +366,18 @@
     return pl.pallas_call(
         functools.partial(store_kernel, n_dp, n_ex),
         out_shape=(jax.ShapeDtypeStruct(tokens.shape, BF16), grad, grad, grad),
-        in_specs=[vmem] + [anywhere] * 4,
+        in_specs=[anywhere] * 5,
         out_specs=(anywhere,) * 4,
         scratch_shapes=[
+            pltpu.VMEM(picks.shape, jnp.int32),
+            pltpu.VMEM((n,) + message, BF16),
+            pltpu.VMEM((n * experts * width // LANES, LANES), F32),
             pltpu.VMEM(rows, BF16),
             pltpu.VMEM(tokens.shape, BF16),
-            pltpu.SemaphoreType.DMA((2,)),
+            pltpu.SemaphoreType.DMA((3,)),
             pltpu.SemaphoreType.DMA((6 * experts,)),
         ],
-        compiler_params=pltpu.CompilerParams(vmem_limit_bytes=8 * 1024 * 1024),
+        compiler_params=pltpu.CompilerParams(vmem_limit_bytes=16 * 1024 * 1024),
     )(picks, back, d_gate, d_up, d_down)
 
 

time: 28.8 us -> 27.6 us (0.958)
  Pallas kernels: 28 us -> 26.8 us
    pallas_call x1, Pallas kernels: 23.7 us -> 23.1 us  [shards(): pl.pallas_call(functools.partial(exchange_kernel, n_dp, n_ex), out_shape=...]
    pallas_call x1, Pallas kernels: 4.33 us -> 3.73 us  [shards(): pl.pallas_call(functools.partial(store_kernel, n_dp, n_ex), out_shape=(ja...]
where the time goes in v6:
time: 27.6 us; the launch traced here: 27.4 us
  Pallas kernels  26.8 us (97%)
  between operations  0.64 us (2%)
    pallas_call x1, Pallas kernels, shards(): pl.pallas_call(functools.partial(exchange_kernel, n_dp, n_ex), out_shape=...  23.1 us
    pallas_call x1, Pallas kernels, shards(): pl.pallas_call(functools.partial(store_kernel, n_dp, n_ex), out_shape=(ja...  3.73 us

profile of v6, /device:TPU:0, one launch (start us, length us, event | category | flops | bytes accessed | tf_op | source)
XLA Modules:
  0.0 27.4 jit_solution(3110977991449431613)
XLA Ops:
  0.6 23.1 %shard_map.102 = (bf16[32,16,128]{2,1,0:T(8,128)(2,1)S(1)}, bf16[2,704,1024]{2,1,0:T(8,128)(2,1)S(1)}, bf16[2,704,1024]{2,1,0:T(8,128)(2,1)S(1)}, bf16[2,704,1024]{2,1,0:T(8,128)(2,1)S(1)}) custom-call(s32[1,16]{1,0:T(1,128)} %picks_hbm.3, f32[1,16]{1,0:T(1,128)} %gates_hbm.1, bf16[128,1024]{1,0:T(8,128)(2,1)} %tokens_hbm.1, bf16[128,1024]{1,0:T(8,128)(2,1)} %cot_hbm.1, ...), custom_call_target="tpu_custom_call" | custom-call | tf_op jit(solution)/shard_map/pallas_call | solution.py:333
  23.7 3.7 %shard_map.103 = (bf16[128,1024]{1,0:T(8,128)(2,1)}, bf16[2,704,1024]{2,1,0:T(8,128)(2,1)}, bf16[2,704,1024]{2,1,0:T(8,128)(2,1)}, bf16[2,704,1024]{2,1,0:T(8,128)(2,1)}) custom-call(s32[1,16]{1,0:T(1,128)} %picks_hbm.3, bf16[32,16,128]{2,1,0:T(8,128)(2,1)S(1)} %get-tuple-element.8.back_in, bf16[2,704,1024]{2,1,0:T(8,128)(2,1)S(1)} %get-tuple-element.9.gate_in, ...), custom_call_target="tpu_custom_call" | custom-call | tf_op jit(solution)/shard_map/pallas_call | solution.py:366

commit v7 on v6

--- a/solution.py
+++ b/solution.py
@@ -46,9 +46,9 @@
     back_out,
     gate_out,
     up_out,
-    down_out,
+    dy_out,
+    hidden_out,
     x_out,
-    dy_out,
     dt_out,
     picks_ref,
     gates_ref,
@@ -94,7 +94,7 @@
             )
         )
     ]
-    for load in loads:
+    for load in loads[:4]:
         load.start()
 
     def wrap(value, size):
@@ -186,6 +186,8 @@
         buf[me] = msg[me]
 
     loads[1].wait()
+    for load in loads[4:]:
+        load.start()
     pack([jnp.dot(selector, tok[...], preferred_element_type=F32)], xmsg)
     pl.semaphore_wait(barrier, n - 1)
     send_chips(xmsg, xbuf, 0)
@@ -233,15 +235,13 @@
     for e in every:
         dt_out[e, 0] = d_gate[e].T.astype(BF16)
         dt_out[e, 1] = d_up[e].T.astype(BF16)
-        dt_out[e, 2] = hidden[e].T.astype(BF16)
+        hidden_out[e] = hidden[e].T.astype(BF16)
 
         def grads(i, carry):
             at = pl.ds(pl.multiple_of(i * block, block), block)
-            for j, (out, other) in enumerate(
-                ((gate_out, x_out), (up_out, x_out), (down_out, dy_out))
-            ):
+            for j, out in enumerate((gate_out, up_out)):
                 out[e, at, :] = jnp.dot(
-                    dt_out[e, j, at, :], other[e], preferred_element_type=F32
+                    dt_out[e, j, at, :], x_out[e], preferred_element_type=F32
                 ).astype(BF16)
             return carry
 
@@ -260,7 +260,8 @@
     back_in,
     gate_in,
     up_in,
-    down_in,
+    dy_in,
+    hidden_in,
     tokens_out,
     gate_out,
     up_out,
@@ -270,29 +271,48 @@
     wide,
     back,
     total,
+    dy,
+    hidden,
+    down,
     sem,
     store_sem,
 ):
-    picks_load = pltpu.make_async_copy(picks_hbm, picks_ref, sem.at[0])
-    picks_load.start()
-    load = pltpu.make_async_copy(back_in, raw, sem.at[2])
-    load.start()
     experts, hidden_units, _ = gate_in.shape
-    half = hidden_units // 2 // 16 * 16
     stores = []
+
+    def store(src, dst):
+        stores.append(pltpu.make_async_copy(src, dst, store_sem.at[len(stores)]))
+        stores[-1].start()
+
+    loads = [
+        pltpu.make_async_copy(src, dst, sem.at[i])
+        for i, (src, dst) in enumerate(
+            ((dy_in, dy), (hidden_in, hidden), (back_in, raw), (picks_hbm, picks_ref))
+        )
+    ]
+    for load in loads:
+        load.start()
     for e in range(experts):
-        for src, dst in ((gate_in, gate_out), (up_in, up_out), (down_in, down_out)):
-            for at in (pl.ds(0, half), pl.ds(half, hidden_units - half)):
-                stores.append(
-                    pltpu.make_async_copy(
-                        src.at[e, at], dst.at[e, at], store_sem.at[len(stores)]
-                    )
-                )
-                stores[-1].start()
+        store(gate_in.at[e], gate_out.at[e])
+        store(up_in.at[e], up_out.at[e])
+    loads[0].wait()
+    loads[1].wait()
+    block = block_of(hidden_units)
+    for e in range(experts):
+
+        def grads(i, carry):
+            at = pl.ds(pl.multiple_of(i * block, block), block)
+            down[e, at, :] = jnp.dot(
+                hidden[e, at, :], dy[e], preferred_element_type=F32
+            ).astype(BF16)
+            return carry
+
+        lax.fori_loop(0, hidden_units // block, grads, 0)
+        store(down.at[e], down_out.at[e])
     token_rows = total.shape[0]
-    load.wait()
+    loads[2].wait()
     unpack(raw, wide, back)
-    picks_load.wait()
+    loads[3].wait()
     picks = picks_ref[...].astype(F32)
     columns = lax.broadcasted_iota(jnp.int32, (picks.shape[1], n_dp * n_ex), 0)
     places = lax.broadcasted_iota(jnp.int32, (picks.shape[1], n_dp * n_ex), 1)
@@ -311,10 +331,9 @@
         ).astype(BF16)
         summed += jnp.dot(chosen, back[e], preferred_element_type=F32)
     total[...] = summed.astype(BF16)
-    stores.append(pltpu.make_async_copy(total, tokens_out, sem.at[1]))
-    stores[-1].start()
-    for store in stores:
-        store.wait()
+    store(total, tokens_out)
+    for copy in stores:
+        copy.wait()
 
 
 def shards(n_dp, n_ex, tokens, cotangent, picks, gates, w_gate, w_up, w_down):
@@ -330,15 +349,16 @@
     weight = pltpu.VMEM((experts, hidden, width), BF16)
     vmem = pl.BlockSpec(memory_space=pltpu.VMEM)
     anywhere = pl.BlockSpec(memory_space=pl.ANY)
-    back, d_gate, d_up, d_down = pl.pallas_call(
+    back, d_gate, d_up, dy, hid = pl.pallas_call(
         functools.partial(exchange_kernel, n_dp, n_ex),
-        out_shape=(pltpu.VMEM((n,) + message, BF16),) + (weight,) * 3,
+        out_shape=(pltpu.VMEM((n,) + message, BF16),)
+        + (weight,) * 2
+        + (pltpu.VMEM(rows, BF16), pltpu.VMEM((experts, hidden, n), BF16)),
         in_specs=[anywhere] * 7,
-        out_specs=(vmem,) * 4,
+        out_specs=(vmem,) * 5,
         scratch_shapes=[
             pltpu.VMEM(rows, BF16),
-            pltpu.VMEM(rows, BF16),
-            pltpu.VMEM((experts, 3, hidden, n), BF16),
+            pltpu.VMEM((experts, 2, hidden, n), BF16),
             pltpu.VMEM(picks.shape, jnp.int32),
             pltpu.VMEM(gates.shape, F32),
             pltpu.VMEM((token_rows, width), BF16),
@@ -366,7 +386,7 @@
     return pl.pallas_call(
         functools.partial(store_kernel, n_dp, n_ex),
         out_shape=(jax.ShapeDtypeStruct(tokens.shape, BF16), grad, grad, grad),
-        in_specs=[anywhere] * 5,
+        in_specs=[anywhere] * 6,
         out_specs=(anywhere,) * 4,
         scratch_shapes=[
             pltpu.VMEM(picks.shape, jnp.int32),
@@ -374,11 +394,14 @@
             pltpu.VMEM((n * experts * width // LANES, LANES), F32),
             pltpu.VMEM(rows, BF16),
             pltpu.VMEM(tokens.shape, BF16),
-            pltpu.SemaphoreType.DMA((3,)),
-            pltpu.SemaphoreType.DMA((6 * experts,)),
+            pltpu.VMEM(rows, BF16),
+            pltpu.VMEM((experts, hidden, n), BF16),
+            weight,
+            pltpu.SemaphoreType.DMA((4,)),
+            pltpu.SemaphoreType.DMA((3 * experts + 1,)),
         ],
         compiler_params=pltpu.CompilerParams(vmem_limit_bytes=16 * 1024 * 1024),
-    )(picks, back, d_gate, d_up, d_down)
+    )(picks, back, d_gate, d_up, dy, hid)
 
 
 def solution(mesh):

time: 27.6 us -> 27.9 us (1.011)
  Pallas kernels: 26.8 us -> 27.1 us
    pallas_call x1, Pallas kernels: 3.73 us -> 4.02 us  [shards(): pl.pallas_call(functools.partial(store_kernel, n_dp, n_ex), out_shape=(ja...]
where the time goes in v7:
time: 27.9 us; the launch traced here: 27.7 us
  Pallas kernels  27.1 us (97%)
  between operations  0.64 us (2%)
    pallas_call x1, Pallas kernels, shards(): pl.pallas_call(functools.partial(exchange_kernel, n_dp, n_ex), out_shape=...  23 us
    pallas_call x1, Pallas kernels, shards(): pl.pallas_call(functools.partial(store_kernel, n_dp, n_ex), out_shape=(ja...  4.02 us

profile of v7, /device:TPU:0, one launch (start us, length us, event | category | flops | bytes accessed | tf_op | source)
XLA Modules:
  0.0 27.7 jit_solution(3202797613786339750)
XLA Ops:
  0.6 23.0 %shard_map.102 = (bf16[32,16,128]{2,1,0:T(8,128)(2,1)S(1)}, bf16[2,704,1024]{2,1,0:T(8,128)(2,1)S(1)}, bf16[2,704,1024]{2,1,0:T(8,128)(2,1)S(1)}, bf16[2,32,1024...) custom-call(s32[1,16]{1,0:T(1,128)} %picks_hbm.3, f32[1,16]{1,0:T(1,128)} %gates_hbm.1, bf16[128,1024]{1,0:T(8,128)(2,1)} %tokens_hbm.1, ...), custom_call_target="tpu_custom_call" | custom-call | tf_op jit(solution)/shard_map/pallas_call | solution.py:352
  23.7 4.0 %shard_map.103 = (bf16[128,1024]{1,0:T(8,128)(2,1)}, bf16[2,704,1024]{2,1,0:T(8,128)(2,1)}, bf16[2,704,1024]{2,1,0:T(8,128)(2,1)}, bf16[2,704,1024]{2,1,0:T(8,128)(2,1)}) custom-call(s32[1,16]{1,0:T(1,128)} %picks_hbm.3, bf16[32,16,128]{2,1,0:T(8,128)(2,1)S(1)} %get-tuple-element.9.back_in, bf16[2,704,1024]{2,1,0:T(8,128)(2,1)S(1)} %get-tuple-element.10.gate_in, ...), custom_call_target="tpu_custom_call" | custom-call | tf_op jit(solution)/shard_map/pallas_call | solution.py:386

commit v8 on v6

--- a/solution.py
+++ b/solution.py
@@ -63,6 +63,8 @@
     xbuf,
     dybuf,
     partmsg,
+    pairbuf,
+    summsg,
     backbuf,
     load_sem,
     send_sem,
@@ -78,7 +80,6 @@
     n_chip = n // cores
     my_core, my_half = lax.rem(my_dp, cores), my_dp // cores
     my_chip = my_half * n_ex + my_ex
-    me = my_core * n_chip + my_chip
 
     loads = [
         pltpu.make_async_copy(src, dst, load_sem.at[i])
@@ -124,8 +125,7 @@
         )
 
     def greet_chip(half, ex):
-        for core in range(cores):
-            greet((half * cores + core, ex))
+        greet((half * cores + my_core, ex))
 
     greet(sibling)
     each_chip(greet_chip)
@@ -175,19 +175,9 @@
         copy.start()
         return copy
 
-    def send_back(msg, buf, slot):
-        def one(half, ex):
-            for core in range(cores):
-                spot = core * n_chip + half * n_ex + ex
-                remote(msg.at[spot], buf.at[me], slot, (half * cores + core, ex)).start()
-
-        each_chip(one)
-        remote(msg.at[(1 - my_core) * n_chip + my_chip], buf.at[me], slot, sibling).start()
-        buf[me] = msg[me]
-
     loads[1].wait()
     pack([jnp.dot(selector, tok[...], preferred_element_type=F32)], xmsg)
-    pl.semaphore_wait(barrier, n - 1)
+    pl.semaphore_wait(barrier, n_chip)
     send_chips(xmsg, xbuf, 0)
     loads[2].wait()
     gate_col = jnp.sum(jnp.where(eye, gates_ref[...], 0.0), axis=1, keepdims=True)
@@ -227,13 +217,27 @@
         ],
         partmsg,
     )
-    send_back(partmsg, backbuf, 4)
+    pair = remote(partmsg.at[1 - my_core], pairbuf, 4, sibling)
+    pair.start()
     hidden_units = wg.shape[1]
     block = block_of(hidden_units)
     for e in every:
         dt_out[e, 0] = d_gate[e].T.astype(BF16)
         dt_out[e, 1] = d_up[e].T.astype(BF16)
         dt_out[e, 2] = hidden[e].T.astype(BF16)
+    pair.wait()
+    own_rows = n_chip * experts * chunks
+    own = wide[pl.ds(pl.multiple_of(my_core * own_rows, own_rows), own_rows), :]
+    summed = own + pairbuf[...].reshape(own.shape).astype(F32)
+    summsg[...] = summed.astype(BF16).reshape(summsg.shape)
+
+    def send_back(half, ex):
+        where = (half * cores + my_core, ex)
+        remote(summsg.at[half * n_ex + ex], backbuf.at[my_chip], 5, where).start()
+
+    each_chip(send_back)
+    backbuf[my_chip] = summsg[my_chip]
+    for e in every:
 
         def grads(i, carry):
             at = pl.ds(pl.multiple_of(i * block, block), block)
@@ -246,15 +250,14 @@
             return carry
 
         lax.fori_loop(0, hidden_units // block, grads, 0)
-    bulk_wait(backbuf, n - 1, recv_sem.at[4])
+    bulk_wait(backbuf, n_chip - 1, recv_sem.at[5])
     back_out[...] = backbuf[...]
     bulk_wait(xbuf.at[0], n_chip - 1, send_sem.at[0])
     bulk_wait(dybuf.at[0], n_chip - 1, send_sem.at[2])
-    bulk_wait(partmsg, n - 1, send_sem.at[4])
+    bulk_wait(summsg, n_chip - 1, send_sem.at[5])
 
 
 def store_kernel(
-    n_dp,
     n_ex,
     picks_hbm,
     back_in,
@@ -289,13 +292,13 @@
                     )
                 )
                 stores[-1].start()
-    token_rows = total.shape[0]
+    token_rows, sources = total.shape[0], back.shape[1]
     load.wait()
     unpack(raw, wide, back)
     picks_load.wait()
     picks = picks_ref[...].astype(F32)
-    columns = lax.broadcasted_iota(jnp.int32, (picks.shape[1], n_dp * n_ex), 0)
-    places = lax.broadcasted_iota(jnp.int32, (picks.shape[1], n_dp * n_ex), 1)
+    columns = lax.broadcasted_iota(jnp.int32, (picks.shape[1], sources), 0)
+    places = lax.broadcasted_iota(jnp.int32, (picks.shape[1], sources), 1)
     summed = jnp.zeros(total.shape, F32)
     for e in range(experts):
         wanted = jnp.where(columns == lax.rem(places, n_ex) * experts + e, 1.0, 0.0)
@@ -305,7 +308,7 @@
             preferred_element_type=F32,
         )[:1]
         chosen = jnp.where(
-            lax.broadcasted_iota(jnp.int32, (token_rows, n_dp * n_ex), 0).astype(F32) == row,
+            lax.broadcasted_iota(jnp.int32, (token_rows, sources), 0).astype(F32) == row,
             1.0,
             0.0,
         ).astype(BF16)
@@ -332,7 +335,7 @@
     anywhere = pl.BlockSpec(memory_space=pl.ANY)
     back, d_gate, d_up, d_down = pl.pallas_call(
         functools.partial(exchange_kernel, n_dp, n_ex),
-        out_shape=(pltpu.VMEM((n,) + message, BF16),) + (weight,) * 3,
+        out_shape=(pltpu.VMEM((n // 2,) + message, BF16),) + (weight,) * 3,
         in_specs=[anywhere] * 7,
         out_specs=(vmem,) * 4,
         scratch_shapes=[
@@ -351,11 +354,13 @@
             pltpu.VMEM((n_ex,) + message, BF16),
             pltpu.VMEM((2, n // 2) + message, BF16),
             pltpu.VMEM((2, n // 2) + message, BF16),
-            pltpu.VMEM((n,) + message, BF16),
-            pltpu.VMEM((n,) + message, BF16),
+            pltpu.VMEM((2, n // 2) + message, BF16),
+            pltpu.VMEM((n // 2,) + message, BF16),
+            pltpu.VMEM((n // 2,) + message, BF16),
+            pltpu.VMEM((n // 2,) + message, BF16),
             pltpu.SemaphoreType.DMA((7,)),
-            pltpu.SemaphoreType.DMA((5,)),
-            pltpu.SemaphoreType.DMA((5,)),
+            pltpu.SemaphoreType.DMA((6,)),
+            pltpu.SemaphoreType.DMA((6,)),
         ],
         compiler_params=pltpu.CompilerParams(
             collective_id=0, has_side_effects=True, vmem_limit_bytes=28 * 1024 * 1024
@@ -364,15 +369,15 @@
 
     grad = jax.ShapeDtypeStruct(w_gate.shape, BF16)
     return pl.pallas_call(
-        functools.partial(store_kernel, n_dp, n_ex),
+        functools.partial(store_kernel, n_ex),
         out_shape=(jax.ShapeDtypeStruct(tokens.shape, BF16), grad, grad, grad),
         in_specs=[anywhere] * 5,
         out_specs=(anywhere,) * 4,
         scratch_shapes=[
             pltpu.VMEM(picks.shape, jnp.int32),
-            pltpu.VMEM((n,) + message, BF16),
-            pltpu.VMEM((n * experts * width // LANES, LANES), F32),
-            pltpu.VMEM(rows, BF16),
+            pltpu.VMEM((n // 2,) + message, BF16),
+            pltpu.VMEM((n * experts * width // LANES // 2, LANES), F32),
+            pltpu.VMEM((experts, n // 2, width), BF16),
             pltpu.VMEM(tokens.shape, BF16),
             pltpu.SemaphoreType.DMA((3,)),
             pltpu.SemaphoreType.DMA((6 * experts,)),

time: 27.6 us -> 27.4 us (level)
  no operation moved by 1% of the time
where the time goes in v8:
time: 27.4 us; the launch traced here: 27.2 us
  Pallas kernels  26.6 us (97%)
  between operations  0.64 us (2%)
    pallas_call x1, Pallas kernels, shards(): pl.pallas_call(functools.partial(exchange_kernel, n_dp, n_ex), out_shape=...  22.9 us
    pallas_call x1, Pallas kernels, shards(): pl.pallas_call(functools.partial(store_kernel, n_ex), out_shape=(jax.Shap...  3.64 us

profile of v8, /device:TPU:0, one launch (start us, length us, event | category | flops | bytes accessed | tf_op | source)
XLA Modules:
  0.0 27.2 jit_solution(4481524509789276124)
XLA Ops:
  0.6 22.9 %shard_map.102 = (bf16[16,16,128]{2,1,0:T(8,128)(2,1)S(1)}, bf16[2,704,1024]{2,1,0:T(8,128)(2,1)S(1)}, bf16[2,704,1024]{2,1,0:T(8,128)(2,1)S(1)}, bf16[2,704,1024]{2,1,0:T(8,128)(2,1)S(1)}) custom-call(s32[1,16]{1,0:T(1,128)} %picks_hbm.3, f32[1,16]{1,0:T(1,128)} %gates_hbm.1, bf16[128,1024]{1,0:T(8,128)(2,1)} %tokens_hbm.1, bf16[128,1024]{1,0:T(8,128)(2,1)} %cot_hbm.1, ...), custom_call_target="tpu_custom_call" | custom-call | tf_op jit(solution)/shard_map/pallas_call | solution.py:336
  23.6 3.6 %shard_map.103 = (bf16[128,1024]{1,0:T(8,128)(2,1)}, bf16[2,704,1024]{2,1,0:T(8,128)(2,1)}, bf16[2,704,1024]{2,1,0:T(8,128)(2,1)}, bf16[2,704,1024]{2,1,0:T(8,128)(2,1)}) custom-call(s32[1,16]{1,0:T(1,128)} %picks_hbm.3, bf16[16,16,128]{2,1,0:T(8,128)(2,1)S(1)} %get-tuple-element.8.back_in, bf16[2,704,1024]{2,1,0:T(8,128)(2,1)S(1)} %get-tuple-element.9.gate_in, ...), custom_call_target="tpu_custom_call" | custom-call | tf_op jit(solution)/shard_map/pallas_call | solution.py:371
